TPU v7x, 32 devices: a whole 2x2x4 slice. The times are simulated.
32 devices in a mesh: fsdp: 8 (over y, x, core), sp: 4 (over z).
Axes of the slice: x: 2, y: 2, z: 4, core: 2. Of those that a mesh axis runs over, the one named last changes fastest.
Arguments:
- tokens: bfloat16 [16, 1024, 2560], P('fsdp', 'sp'), may hold values from -6 to 6
- segments: int32 [16, 1024], P('fsdp'), may hold values from 0 to 24, as said below
- w_query: float32 [2560, 2560], P('fsdp'), may hold values from -0.125 to 0.125
- w_key: float32 [2560, 640], P('fsdp'), may hold values from -0.125 to 0.125
- w_value: float32 [2560, 640], P('fsdp'), may hold values from -0.125 to 0.125
- w_out: float32 [2560, 2560], P('fsdp'), may hold values from -0.3125 to 0.3125
- w_gate: float32 [2560, 7168], P('fsdp'), may hold values from -0.125 to 0.125
- w_up: float32 [2560, 7168], P('fsdp'), may hold values from -0.125 to 0.125
- w_down: float32 [7168, 2560], P('fsdp'), may hold values from -0.0625 to 0.0625
- gain_attn: float32 [2560], P('fsdp'), may hold values from 0.5 to 1.5
- gain_mlp: float32 [2560], P('fsdp'), may hold values from 0.5 to 1.5
- cotangent: bfloat16 [16, 1024, 2560], P('fsdp', 'sp'), may hold values from -6 to 6
Outputs:
- layer_out: bfloat16 [16, 1024, 2560], P('fsdp', 'sp')
- grad_tokens: float32 [16, 1024, 2560], P('fsdp', 'sp')
- grad_w_query: float32 [2560, 2560], P('fsdp')
- grad_w_key: float32 [2560, 640], P('fsdp')
- grad_w_value: float32 [2560, 640], P('fsdp')
- grad_w_out: float32 [2560, 2560], P('fsdp')
- grad_w_gate: float32 [2560, 7168], P('fsdp')
- grad_w_up: float32 [2560, 7168], P('fsdp')
- grad_w_down: float32 [7168, 2560], P('fsdp')
- grad_gain_attn: float32 [2560], P('fsdp')
- grad_gain_mlp: float32 [2560], P('fsdp')
Inputs may be any that keep to these rules, and one draw needn't show every extreme that they name: `segments`: in every sequence the segment ids start at 0, never fall from one position to the next, and rise by at most one; equal ids mark one document.
All inputs are finite; a program needn't handle non-finite values.
Results may differ from a plain program's by a relative error of at most 0.015.
Values may be sent and summed in bfloat16 or wider, within the bound.
No kernel may reach another device: no remote copies, remote signals or barrier semaphores. Data moves between devices by JAX's collectives and lax.ppermute only.
A program may use at most 704 MiB of HBM per device.

v0:
```python
import math

import jax
import jax.numpy as jnp
from jax import lax
from jax.sharding import PartitionSpec as P

HEADS = 32
KV_HEADS = 8
HEAD_DIM = 80
SEQ_LEN = 1024


epsilon = 1e-05
rope_base = 1000000.0


def contract_last(left, right):
    return lax.dot_general(
        left, right, (((1,), (1,)), ((), ())), preferred_element_type=jnp.float32
    )


def contract_first(left, right):
    return lax.dot_general(
        left, right, (((0,), (0,)), ((), ())), preferred_element_type=jnp.float32
    )


def turn_pairs(field, cosine, sine, direction):
    half = field.shape[-1] // 2
    leading = field[..., :half]
    trailing = field[..., half:]
    return jnp.concatenate(
        [
            leading * cosine - direction * trailing * sine,
            trailing * cosine + direction * leading * sine,
        ],
        axis=-1,
    )


def norm_back(grad_normed, unit, rstd, gain):
    scaled = grad_normed * gain
    return rstd * (scaled - unit * jnp.mean(scaled * unit, axis=-1, keepdims=True))


def local(
    tokens,
    segments,
    w_query,
    w_key,
    w_value,
    w_out,
    w_gate,
    w_up,
    w_down,
    gain_attn,
    gain_mlp,
    cotangent,
):
    seqs_here, local_len, width = tokens.shape
    n_parts = lax.axis_size("sp")
    heads_here = HEADS // n_parts
    kv_here = KV_HEADS // n_parts
    group = HEADS // KV_HEADS
    rows = seqs_here * local_len
    scale = 1.0 / math.sqrt(HEAD_DIM)
    block = min(512, SEQ_LEN)
    blocks = SEQ_LEN // block
    half = HEAD_DIM // 2
    freqs = jnp.power(
        jnp.float32(rope_base), -jnp.arange(half, dtype=jnp.float32) * (2.0 / HEAD_DIM)
    )
    positions = (lax.axis_index("sp") * local_len + jnp.arange(local_len, dtype=jnp.int32)).astype(
        jnp.float32
    )
    angle = positions[:, None] * freqs[None, :]
    cosine = jnp.cos(angle)[:, None, :]
    sine = jnp.sin(angle)[:, None, :]

    def score_block(query_block, keys, segment, start):
        scores = (
            jnp.einsum("qkgd,skd->kgqs", query_block, keys, preferred_element_type=jnp.float32)
            * scale
        )
        row_pos = start + jnp.arange(block)
        col_pos = jnp.arange(SEQ_LEN)
        seg_rows = segment[start : start + block]
        allowed = (seg_rows[:, None] == segment[None, :]) & (row_pos[:, None] >= col_pos[None, :])
        return (scores, allowed)

    def attend_forward(packed):
        query, keys, values, segment = packed
        outputs = []
        totals = []
        for index in range(blocks):
            start = index * block
            scores, allowed = score_block(query[start : start + block], keys, segment, start)
            masked = jnp.where(allowed, scores, -1e30)
            topmost = jnp.max(masked, axis=-1, keepdims=True)
            expo = jnp.exp(masked - topmost)
            summed = jnp.sum(expo, axis=-1, keepdims=True)
            probs = expo / summed
            outputs.append(
                jnp.einsum(
                    "kgqs,skd->qkgd",
                    probs.astype(jnp.bfloat16),
                    values,
                    preferred_element_type=jnp.float32,
                )
            )
            totals.append(topmost[..., 0] + jnp.log(summed[..., 0]))
        output = jnp.concatenate(outputs, axis=0).astype(jnp.bfloat16)
        return (output.reshape(SEQ_LEN, heads_here * HEAD_DIM), jnp.concatenate(totals, axis=-1))

    def attend_backward(packed):
        query, keys, values, grad_head, logsum, segment = packed
        grad_keys = jnp.zeros((SEQ_LEN, kv_here, HEAD_DIM), jnp.float32)
        grad_values = jnp.zeros((SEQ_LEN, kv_here, HEAD_DIM), jnp.float32)
        grad_queries = []
        for index in range(blocks):
            start = index * block
            query_block = query[start : start + block]
            grad_block = grad_head[start : start + block]
            scores, allowed = score_block(query_block, keys, segment, start)
            probs = jnp.exp(
                jnp.where(allowed, scores - logsum[..., start : start + block, None], -1e30)
            )
            grad_probs = jnp.einsum(
                "qkgd,skd->kgqs", grad_block, values, preferred_element_type=jnp.float32
            )
            delta = jnp.sum(probs * grad_probs, axis=-1, keepdims=True)
            grad_scores = (probs * (grad_probs - delta)).astype(jnp.bfloat16)
            grad_queries.append(
                jnp.einsum("kgqs,skd->qkgd", grad_scores, keys, preferred_element_type=jnp.float32)
                * scale
            )
            grad_keys = (
                grad_keys
                + jnp.einsum(
                    "kgqs,qkgd->skd", grad_scores, query_block, preferred_element_type=jnp.float32
                )
                * scale
            )
            grad_values = grad_values + jnp.einsum(
                "kgqs,qkgd->skd",
                probs.astype(jnp.bfloat16),
                grad_block,
                preferred_element_type=jnp.float32,
            )
        grad_query = (
            jnp.concatenate(grad_queries, axis=0)
            .astype(jnp.bfloat16)
            .reshape(SEQ_LEN, heads_here * HEAD_DIM)
        )
        return (
            grad_query,
            grad_keys.astype(jnp.bfloat16).reshape(SEQ_LEN, kv_here * HEAD_DIM),
            grad_values.astype(jnp.bfloat16).reshape(SEQ_LEN, kv_here * HEAD_DIM),
        )

    attn_full = (
        lax.all_gather(w_query.astype(jnp.bfloat16), "fsdp", axis=0, tiled=True),
        lax.all_gather(w_key.astype(jnp.bfloat16), "fsdp", axis=0, tiled=True),
        lax.all_gather(w_value.astype(jnp.bfloat16), "fsdp", axis=0, tiled=True),
        lax.all_gather(w_out.astype(jnp.bfloat16), "fsdp", axis=0, tiled=True),
        lax.all_gather(gain_attn.astype(jnp.bfloat16), "fsdp", axis=0, tiled=True),
    )
    query_full, key_full, value_full, out_full, gain_one_low = attn_full
    gain_one = gain_one_low.astype(jnp.float32)
    inputs = tokens.reshape(rows, width).astype(jnp.float32)
    rstd_one = lax.rsqrt(jnp.mean(inputs * inputs, axis=-1, keepdims=True) + epsilon)
    unit_one = inputs * rstd_one
    normed_one = (unit_one * gain_one).astype(jnp.bfloat16)
    query_lin = jnp.dot(normed_one, query_full, preferred_element_type=jnp.float32).reshape(
        seqs_here, local_len, HEADS, HEAD_DIM
    )
    key_lin = jnp.dot(normed_one, key_full, preferred_element_type=jnp.float32).reshape(
        seqs_here, local_len, KV_HEADS, HEAD_DIM
    )
    query_tok = (
        turn_pairs(query_lin, cosine, sine, 1.0)
        .astype(jnp.bfloat16)
        .reshape(seqs_here, local_len, HEADS * HEAD_DIM)
    )
    key_tok = (
        turn_pairs(key_lin, cosine, sine, 1.0)
        .astype(jnp.bfloat16)
        .reshape(seqs_here, local_len, KV_HEADS * HEAD_DIM)
    )
    value_tok = (
        jnp.dot(normed_one, value_full, preferred_element_type=jnp.float32)
        .astype(jnp.bfloat16)
        .reshape(seqs_here, local_len, KV_HEADS * HEAD_DIM)
    )
    query_head, key_head, value_head = (
        lax.all_to_all(query_tok, "sp", split_axis=2, concat_axis=1, tiled=True),
        lax.all_to_all(key_tok, "sp", split_axis=2, concat_axis=1, tiled=True),
        lax.all_to_all(value_tok, "sp", split_axis=2, concat_axis=1, tiled=True),
    )
    query_head = query_head.reshape(seqs_here, SEQ_LEN, kv_here, group, HEAD_DIM)
    key_head = key_head.reshape(seqs_here, SEQ_LEN, kv_here, HEAD_DIM)
    value_head = value_head.reshape(seqs_here, SEQ_LEN, kv_here, HEAD_DIM)
    output_head, logsum_head = lax.map(attend_forward, (query_head, key_head, value_head, segments))
    attn_tok = lax.all_to_all(output_head, "sp", split_axis=1, concat_axis=2, tiled=True)
    attn_flat = attn_tok.reshape(rows, HEADS * HEAD_DIM)
    resid = inputs + jnp.dot(attn_flat, out_full, preferred_element_type=jnp.float32)
    mlp_full = (
        lax.all_gather(w_gate.astype(jnp.bfloat16), "fsdp", axis=0, tiled=True),
        lax.all_gather(w_up.astype(jnp.bfloat16), "fsdp", axis=0, tiled=True),
        lax.all_gather(w_down.astype(jnp.bfloat16), "fsdp", axis=0, tiled=True),
        lax.all_gather(gain_mlp.astype(jnp.bfloat16), "fsdp", axis=0, tiled=True),
    )
    gate_full, up_full, down_full, gain_two_low = mlp_full
    gain_two = gain_two_low.astype(jnp.float32)
    rstd_two = lax.rsqrt(jnp.mean(resid * resid, axis=-1, keepdims=True) + epsilon)
    unit_two = resid * rstd_two
    normed_two = (unit_two * gain_two).astype(jnp.bfloat16)
    gate_pre = jnp.dot(normed_two, gate_full, preferred_element_type=jnp.float32)
    up_pre = jnp.dot(normed_two, up_full, preferred_element_type=jnp.float32)
    sigma = jax.nn.sigmoid(gate_pre)
    silu_value = gate_pre * sigma
    hidden = (silu_value * up_pre).astype(jnp.bfloat16)
    layer_out = (resid + jnp.dot(hidden, down_full, preferred_element_type=jnp.float32)).astype(
        jnp.bfloat16
    )
    mlp_back = (
        lax.all_gather(w_gate.astype(jnp.bfloat16), "fsdp", axis=0, tiled=True),
        lax.all_gather(w_up.astype(jnp.bfloat16), "fsdp", axis=0, tiled=True),
        lax.all_gather(w_down.astype(jnp.bfloat16), "fsdp", axis=0, tiled=True),
        lax.all_gather(gain_mlp.astype(jnp.bfloat16), "fsdp", axis=0, tiled=True),
    )
    attn_back = (
        lax.all_gather(w_query.astype(jnp.bfloat16), "fsdp", axis=0, tiled=True),
        lax.all_gather(w_key.astype(jnp.bfloat16), "fsdp", axis=0, tiled=True),
        lax.all_gather(w_value.astype(jnp.bfloat16), "fsdp", axis=0, tiled=True),
        lax.all_gather(w_out.astype(jnp.bfloat16), "fsdp", axis=0, tiled=True),
        lax.all_gather(gain_attn.astype(jnp.bfloat16), "fsdp", axis=0, tiled=True),
    )
    gate_back, up_back, down_back, gain_two_back = mlp_back
    query_back, key_back, value_back, out_back, gain_one_back = attn_back
    grad_low = cotangent.reshape(rows, width)
    grad_out = grad_low.astype(jnp.float32)
    grad_hidden = contract_last(grad_low, down_back)
    grad_gate = (grad_hidden * up_pre * sigma * (1.0 + gate_pre * (1.0 - sigma))).astype(
        jnp.bfloat16
    )
    grad_up = (grad_hidden * silu_value).astype(jnp.bfloat16)
    grad_normed_two = contract_last(grad_gate, gate_back) + contract_last(grad_up, up_back)
    grad_gain_two = jnp.sum(grad_normed_two * unit_two, axis=0)
    grad_resid = grad_out + norm_back(
        grad_normed_two, unit_two, rstd_two, gain_two_back.astype(jnp.float32)
    )
    shard_gate = lax.psum_scatter(
        contract_first(normed_two, grad_gate), "fsdp", scatter_dimension=0, tiled=True
    )
    shard_up = lax.psum_scatter(
        contract_first(normed_two, grad_up), "fsdp", scatter_dimension=0, tiled=True
    )
    shard_down = lax.psum_scatter(
        contract_first(hidden, grad_low), "fsdp", scatter_dimension=0, tiled=True
    )
    grad_branch = grad_resid.astype(jnp.bfloat16)
    grad_attn = (
        contract_last(grad_branch, out_back)
        .astype(jnp.bfloat16)
        .reshape(seqs_here, local_len, HEADS * HEAD_DIM)
    )
    term_out = contract_first(attn_flat, grad_branch)
    grad_head = lax.all_to_all(grad_attn, "sp", split_axis=2, concat_axis=1, tiled=True)
    grad_head = grad_head.reshape(seqs_here, SEQ_LEN, kv_here, group, HEAD_DIM)
    grad_query_head, grad_key_head, grad_value_head = lax.map(
        attend_backward, (query_head, key_head, value_head, grad_head, logsum_head, segments)
    )
    grad_query_tok, grad_key_tok, grad_value_tok = (
        lax.all_to_all(grad_query_head, "sp", split_axis=1, concat_axis=2, tiled=True),
        lax.all_to_all(grad_key_head, "sp", split_axis=1, concat_axis=2, tiled=True),
        lax.all_to_all(grad_value_head, "sp", split_axis=1, concat_axis=2, tiled=True),
    )
    grad_query_lin = (
        turn_pairs(
            grad_query_tok.reshape(seqs_here, local_len, HEADS, HEAD_DIM).astype(jnp.float32),
            cosine,
            sine,
            -1.0,
        )
        .astype(jnp.bfloat16)
        .reshape(rows, HEADS * HEAD_DIM)
    )
    grad_key_lin = (
        turn_pairs(
            grad_key_tok.reshape(seqs_here, local_len, KV_HEADS, HEAD_DIM).astype(jnp.float32),
            cosine,
            sine,
            -1.0,
        )
        .astype(jnp.bfloat16)
        .reshape(rows, KV_HEADS * HEAD_DIM)
    )
    grad_value = grad_value_tok.reshape(rows, KV_HEADS * HEAD_DIM)
    grad_normed_one = (
        contract_last(grad_query_lin, query_back)
        + contract_last(grad_key_lin, key_back)
        + contract_last(grad_value, value_back)
    )
    grad_gain_one = jnp.sum(grad_normed_one * unit_one, axis=0)
    grad_inputs = grad_resid + norm_back(
        grad_normed_one, unit_one, rstd_one, gain_one_back.astype(jnp.float32)
    )
    term_query = contract_first(normed_one, grad_query_lin)
    term_key = contract_first(normed_one, grad_key_lin)
    term_value = contract_first(normed_one, grad_value)
    shard_query, shard_key, shard_value, shard_out, shard_gain_one, shard_gain_two = (
        lax.psum_scatter(term_query, "fsdp", scatter_dimension=0, tiled=True),
        lax.psum_scatter(term_key, "fsdp", scatter_dimension=0, tiled=True),
        lax.psum_scatter(term_value, "fsdp", scatter_dimension=0, tiled=True),
        lax.psum_scatter(term_out, "fsdp", scatter_dimension=0, tiled=True),
        lax.psum_scatter(grad_gain_one, "fsdp", scatter_dimension=0, tiled=True),
        lax.psum_scatter(grad_gain_two, "fsdp", scatter_dimension=0, tiled=True),
    )
    summed = lax.psum(
        (
            shard_query,
            shard_key,
            shard_value,
            shard_out,
            shard_gate,
            shard_up,
            shard_down,
            shard_gain_one,
            shard_gain_two,
        ),
        "sp",
    )
    return (
        layer_out.reshape(seqs_here, local_len, width),
        grad_inputs.reshape(seqs_here, local_len, width),
        summed[0],
        summed[1],
        summed[2],
        summed[3],
        summed[4],
        summed[5],
        summed[6],
        summed[7],
        summed[8],
    )


def solution(mesh):
    return jax.shard_map(
        local,
        mesh=mesh,
        in_specs=(
            P("fsdp", "sp", None),
            P("fsdp", None),
            P("fsdp", None),
            P("fsdp", None),
            P("fsdp", None),
            P("fsdp", None),
            P("fsdp", None),
            P("fsdp", None),
            P("fsdp", None),
            P("fsdp"),
            P("fsdp"),
            P("fsdp", "sp", None),
        ),
        out_specs=(
            P("fsdp", "sp", None),
            P("fsdp", "sp", None),
            P("fsdp", None),
            P("fsdp", None),
            P("fsdp", None),
            P("fsdp", None),
            P("fsdp", None),
            P("fsdp", None),
            P("fsdp", None),
            P("fsdp"),
            P("fsdp"),
        ),
        check_vma=False,
    )
```

profile of v0, /device:TPU:0, one launch (start us, length us, event | category | flops | bytes accessed | tf_op | source)
XLA Modules:
  0.0 4134.8 jit_solution(15957405143625487261)
XLA Ops:
  93.2 65.1 %all-gather.12.cloned.1.call-done = bf16[2560,2560]{1,0:T(8,128)(2,1)} async-done(((bf16[320,2560]{1,0:T(8,128)(2,1)}), bf16[2560,2560]{1,0:T(8,128)(2,1)}) %all-gather.12.cloned.1.call-update) | async-done | bytes 13107216 | tf_op jit(solution)/shard_map/all_gather | solution.py:164
  222.9 51.3 %all-to-all-done.2 = bf16[2,256,2560]{1,0,2:T(2,128)(2,1)S(1)} async-done(((bf16[2,256,2560]{1,0,2:T(2,128)(2,1)}), bf16[2,256,2560]{1,0,2:T(2,128)(2,1)S(1)}, u32[]{:S(2)}, u32[]{:S(2)}) %all-to-all-start.2) | async-done | bytes 2621472 | tf_op jit(solution)/shard_map/all_to_all | solution.py:198
  283.9 76.0 %while.26 = (s32[]{:T(128)}, bf16[2,1024,640]{1,2,0:T(8,128)(2,1)}, f32[2,2,4,1024]{3,2,1,0:T(4,128)S(1)}, bf16[2,1024,2,80]{1,3,2,0:T(8,128)(2,1)}, s32[2,1024]...) while((s32[]{:T(128)}, bf16[2,1024,640]{1,2,0:T(8,128)(2,1)}, ...), condition=%wide.region_6.7_spmd, body=%wide.region_1.6_spmd.sunk | while | flops 2791440896 | bytes 114391720 | solution.py:205
  372.7 57.0 %all-to-all-done.3 = bf16[2,1024,640]{2,0,1:T(2,128)(2,1)} async-done(((bf16[2,1024,640]{2,0,1:T(2,128)(2,1)}), bf16[2,1024,640]{2,0,1:T(2,128)(2,1)}, u32[]{:S(2)}, u32[]{:S(2)}) %all-to-all-start.3) | async-done | bytes 2621472 | tf_op jit(solution)/shard_map/all_to_all | solution.py:206
  476.1 113.5 %all-gather.18.cloned.1.call-done = bf16[2560,7168]{1,0:T(8,128)(2,1)} async-done(((bf16[320,7168]{1,0:T(8,128)(2,1)}), bf16[2560,7168]{1,0:T(8,128)(2,1)}) %all-gather.18.cloned.1.call-update) | async-done | bytes 36700176 | tf_op jit(solution)/shard_map/all_gather | solution.py:211
  589.6 28.0 fusion.121
  617.6 149.7 %all-gather.20.cloned.1.call-done = bf16[7168,2560]{1,0:T(8,128)(2,1)} async-done(((bf16[896,2560]{1,0:T(8,128)(2,1)}), bf16[7168,2560]{1,0:T(8,128)(2,1)}) %all-gather.20.cloned.1.call-update) | async-done | bytes 36700176 | tf_op jit(solution)/shard_map/all_gather | solution.py:212
  767.3 36.7 multiply_convert_fusion
  804.1 26.4 fusion.122
  830.5 28.6 multiply_reduce_fusion
  884.6 59.8 %all-to-all-done.4 = bf16[2,256,2560]{1,0,2:T(2,128)(2,1)S(1)} async-done(((bf16[2,256,2560]{1,0,2:T(2,128)(2,1)}), bf16[2,256,2560]{1,0,2:T(2,128)(2,1)S(1)}, u32[]{:S(2)}, u32[]{:S(2)}) %all-to-all-start.4) | async-done | bytes 2621472 | tf_op jit(solution)/shard_map/all_to_all | solution.py:271
  955.2 206.6 %while.27 = (s32[]{:T(128)}, bf16[2,1024,640]{1,2,0:T(8,128)(2,1)}, bf16[2,1024,160]{1,2,0:T(8,128)(2,1)}, bf16[2,1024,160]{1,2,0:T(8,128)(2,1)}, bf16[2,1024,2,...) while((s32[]{:T(128)}, bf16[2,1024,640]{1,2,0:T(8,128)(2,1)}, ...), condition=%wide.region_12.13_spmd, body=%wide.region_9.12_spmd.sunk | while | flops 6844604928 | bytes 356976224 | solution.py:273
  1165.5 29.9 all_to_all.108
  1210.4 29.1 all_to_all.109
  1273.1 63.6 %all_to_all.110 = bf16[2,1024,640]{2,0,1:T(2,128)(2,1)} all-to-all(bf16[2,1024,640]{2,0,1:T(2,128)(2,1)} %copy.101), channel_id=1, replica_groups=mesh['fsdp'=8,'sp'=4] {'sp'}, dimensions={1} | all-to-all | bytes 5242880 | tf_op jit(solution)/shard_map/all_to_all | solution.py:277
  1374.1 34.3 fusion.128
  1408.5 34.1 fusion.129
  1444.4 32.2 fusion.130
  1502.0 166.1 %reduce-scatter.8.cloned.1.call-done = f32[320,2560]{1,0:T(8,128)} async-done(((f32[2560,2560]{1,0:T(8,128)}), f32[320,2560]{1,0:T(8,128)}) %reduce-scatter.8.cloned.1.call-update) | async-done | bytes 3276816 | tf_op jit(solution)/shard_map/reduce_scatter | solution.py:315
  1668.1 416.4 %reduce-scatter.16.cloned.1.call-done = f32[320,7168]{1,0:T(8,128)} async-done(((f32[2560,7168]{1,0:T(8,128)}), f32[320,7168]{1,0:T(8,128)}) %reduce-scatter.16.cloned.1.call-update) | async-done | bytes 9175056 | tf_op jit(solution)/shard_map/reduce_scatter | solution.py:255
  2084.5 416.6 %reduce-scatter.18.cloned.1.call-done = f32[320,7168]{1,0:T(8,128)} async-done(((f32[2560,7168]{1,0:T(8,128)}), f32[320,7168]{1,0:T(8,128)}) %reduce-scatter.18.cloned.1.call-update) | async-done | bytes 9175056 | tf_op jit(solution)/shard_map/reduce_scatter | solution.py:258
  2501.1 416.4 %reduce-scatter.20.cloned.1.call-done = f32[896,2560]{1,0:T(8,128)} async-done(((f32[7168,2560]{1,0:T(8,128)}), f32[896,2560]{1,0:T(8,128)}) %reduce-scatter.20.cloned.1.call-update) | async-done | bytes 9175056 | tf_op jit(solution)/shard_map/reduce_scatter | solution.py:261
  2918.1 30.6 add_convert_fusion
  3012.9 1091.2 %all-reduce.10.cloned.1.call-done = (f32[320,2560]{1,0:T(8,128)}, f32[320,640]{1,0:T(8,128)}, f32[320,640]{1,0:T(8,128)}, f32[320,2560]{1,0:T(8,128)}, f32[320,7...) async-done(((f32[320,2560]{1,0:T(8,128)}, f32[320,640]{1,0:T(8,128)}, f32[320,640]{1,0:T(8,128)}, f32[320,2560]{1,0:T(8,128)}, f32[320,7168]{1,0:T(8,128)}, ...) | async-done | bytes 35717136 | tf_op jit(solution)/shard_map/psum | solution.py:322
  (375 shorter events, 740.4 us)
Async XLA Ops:
  7.2 59.8 %all-gather.10.cloned.1.call-start = ((), (), s32[]{:S(2)}) async-start(), calls=%async_computation.16 | async-start | bytes 3686400 | tf_op jit(solution)/shard_map/all_gather | solution.py:165
  9.3 77.2 %all-gather.8.cloned.1.call-start = ((), (), s32[]{:S(2)}) async-start(), calls=%async_computation.15 | async-start | bytes 3686400 | tf_op jit(solution)/shard_map/all_gather | solution.py:166
  11.4 147.0 %all-gather.12.cloned.1.call-start = ((), (), s32[]{:S(2)}) async-start(), calls=%async_computation.17 | async-start | bytes 14745600 | tf_op jit(solution)/shard_map/all_gather | solution.py:164
  12.8 423.3 %all-gather.14.cloned.1.call-start = ((), (), s32[]{:S(2)}) async-start(), calls=%async_computation.18 | async-start | bytes 14745600 | tf_op jit(solution)/shard_map/all_gather | solution.py:167
  16.2 433.9 %all-gather.16.cloned.1.call-start = ((), (), s32[]{:S(2)}) async-start(), calls=%async_computation.19 | async-start | bytes 41287680 | tf_op jit(solution)/shard_map/all_gather | solution.py:210
  22.7 566.9 %all-gather.18.cloned.1.call-start = ((), (), s32[]{:S(2)}) async-start(), calls=%async_computation.20 | async-start | bytes 41287680 | tf_op jit(solution)/shard_map/all_gather | solution.py:211
  29.2 738.1 %all-gather.20.cloned.1.call-start = ((), (), s32[]{:S(2)}) async-start(), calls=%async_computation.21 | async-start | bytes 41287680 | tf_op jit(solution)/shard_map/all_gather | solution.py:212
  64.9 126.7 %copy-start.34 = (f32[256,40]{0,1:T(8,128)}, f32[256,40]{0,1:T(8,128)S(1)}, u32[]{:S(2)}) copy-start(f32[256,40]{0,1:T(8,128)S(1)} %get-tuple-element.196) | copy-start | bytes 122884
  79.3 97.2 %all-to-all-start.1 = ((bf16[2,256,640]{1,0,2:T(2,128)(2,1)}), bf16[2,256,640]{1,0,2:T(2,128)(2,1)S(1)}, u32[]{:S(2)}, u32[]{:S(2)}) async-start(bf16[2,256,640]{1,0,2:T(2,128)(2,1)} %copy.92), calls=%async_computation.1 | async-start | bytes 1310720 | tf_op jit(solution)/shard_map/all_to_all | solution.py:199
  176.5 33.4 all-to-all-start
  209.9 64.4 %all-to-all-start.2 = ((bf16[2,256,2560]{1,0,2:T(2,128)(2,1)}), bf16[2,256,2560]{1,0,2:T(2,128)(2,1)S(1)}, u32[]{:S(2)}, u32[]{:S(2)}) async-start(bf16[2,256,2560]{1,0,2:T(2,128)(2,1)} %copy.95), calls=%async_computation.2 | async-start | bytes 5242880 | tf_op jit(solution)/shard_map/all_to_all | solution.py:198
  367.7 62.0 %all-to-all-start.3 = ((bf16[2,1024,640]{2,0,1:T(2,128)(2,1)}), bf16[2,1024,640]{2,0,1:T(2,128)(2,1)}, u32[]{:S(2)}, u32[]{:S(2)}) async-start(bf16[2,1024,640]{2,0,1:T(2,128)(2,1)} %copy.97), calls=%async_computation.3 | async-start | bytes 5242880 | tf_op jit(solution)/shard_map/all_to_all | solution.py:206
  372.6 74.5 %copy-start.50 = (f32[2560]{0:T(1024)}, f32[2560]{0:T(1024)S(1)}, u32[]{:S(2)}) copy-start(f32[2560]{0:T(1024)S(1)} %convert_element_type.228) | copy-start | bytes 30724
  450.0 139.6 %copy-start.14 = (bf16[512,2560]{1,0:T(8,128)(2,1)}, bf16[512,2560]{1,0:T(8,128)(2,1)S(1)}, u32[]{:S(2)}) copy-start(bf16[512,2560]{1,0:T(8,128)(2,1)S(1)} %multiply_convert_fusion.3) | copy-start | bytes 7864324
  880.0 64.4 %all-to-all-start.4 = ((bf16[2,256,2560]{1,0,2:T(2,128)(2,1)}), bf16[2,256,2560]{1,0,2:T(2,128)(2,1)S(1)}, u32[]{:S(2)}, u32[]{:S(2)}) async-start(bf16[2,256,2560]{1,0,2:T(2,128)(2,1)} %copy.99), calls=%async_computation.4 | async-start | bytes 5242880 | tf_op jit(solution)/shard_map/all_to_all | solution.py:271
  884.5 592.2 %reduce-scatter.10.cloned.1.call-start = ((), (), s32[]{:S(2)}) async-start(), calls=%async_computation.23 | async-start | bytes 7372800 | tf_op jit(solution)/shard_map/reduce_scatter | solution.py:316
  1062.9 42.4 %copy-start.23 = (f32[2,4,512]{2,1,0:T(4,128)}, f32[2,4,512]{2,1,0:T(4,128)S(1)}, u32[]{:S(2)}) copy-start(f32[2,4,512]{2,1,0:T(4,128)S(1)} %get-tuple-element.339) | copy-start | bytes 49156 | tf_op jit(solution)/shard_map/while
  1207.3 269.4 %reduce-scatter.12.cloned.1.call-start = ((), (), s32[]{:S(2)}) async-start(), calls=%async_computation.24 | async-start | bytes 7372800 | tf_op jit(solution)/shard_map/reduce_scatter | solution.py:317
  1250.2 251.8 %reduce-scatter.14.cloned.1.call-start = ((), (), s32[]{:S(2)}) async-start(), calls=%async_computation.25 | async-start | bytes 29491200 | tf_op jit(solution)/shard_map/reduce_scatter | solution.py:318
  1265.6 402.4 %reduce-scatter.8.cloned.1.call-start = ((), (), s32[]{:S(2)}) async-start(), calls=%async_computation.22 | async-start | bytes 29491200 | tf_op jit(solution)/shard_map/reduce_scatter | solution.py:315
  1372.2 712.3 %reduce-scatter.16.cloned.1.call-start = ((), (), s32[]{:S(2)}) async-start(), calls=%async_computation.26 | async-start | bytes 82575360 | tf_op jit(solution)/shard_map/reduce_scatter | solution.py:255
  1408.5 1092.6 %reduce-scatter.18.cloned.1.call-start = ((), (), s32[]{:S(2)}) async-start(), calls=%async_computation.27 | async-start | bytes 82575360 | tf_op jit(solution)/shard_map/reduce_scatter | solution.py:258
  1442.7 1474.9 %reduce-scatter.20.cloned.1.call-start = ((), (), s32[]{:S(2)}) async-start(), calls=%async_computation.28 | async-start | bytes 82575360 | tf_op jit(solution)/shard_map/reduce_scatter | solution.py:261
  1476.6 2627.5 %all-reduce.10.cloned.1.call-start = ((), (), s32[]{:S(2)}) async-start(), calls=%async_computation.29 | async-start | bytes 71434240 | tf_op jit(solution)/shard_map/psum | solution.py:322
  (79 other events, 865.9 us)
Sparse Core Ops, SparseCore 0:
  10.5 35.5 all-gather.9
  48.5 32.8 all-gather.7
  83.9 74.3 all-gather.11
  160.1 74.3 all-gather.13
  236.8 175.1 all-gather.15
  414.4 175.1 all-gather.17
  592.1 175.1 all-gather.19
  1207.4 61.1 reduce-scatter.9
  1273.1 62.9 reduce-scatter.11
  1339.6 162.3 reduce-scatter.13
  1505.7 162.3 reduce-scatter.7
  1671.7 412.7 reduce-scatter.15
  2088.2 412.7 reduce-scatter.17
  2504.7 412.8 reduce-scatter.19
  2920.8 1183.2 all-reduce.9
where the time goes:
time: 4150 us; the launch traced here: 4130 us
  waiting for transfers between devices  3030 us (73%)
  matrix products  580 us (14%)
  blocking collectives  185 us (4%)
  local copies, waits for them, and re-layouts  173 us (4%)
  other arithmetic  126 us (3%)
    psum x1, waiting for transfers between devices, local(): lax.psum((shard_query, shard_key, shard_value, shard_out, shard_gate, sha...  1090 us
    reduce_scatter x1, waiting for transfers between devices, local(): lax.psum_scatter(contract_first(normed_two, grad_up), 'fsdp', scatter_dim...  417 us
    reduce_scatter x1, waiting for transfers between devices, local(): lax.psum_scatter(contract_first(hidden, grad_low), 'fsdp', scatter_dimens...  416 us
    reduce_scatter x1, waiting for transfers between devices, local(): lax.psum_scatter(contract_first(normed_two, grad_gate), 'fsdp', scatter_d...  416 us
    reduce_scatter x1, waiting for transfers between devices, local(): lax.psum_scatter(term_query, 'fsdp', scatter_dimension=0, tiled=True)  166 us
    all_gather x1, waiting for transfers between devices, local(): lax.all_gather(w_down.astype(jnp.bfloat16), 'fsdp', axis=0, tiled=True)  150 us
    dot_general x7, matrix products, contract_first(): lax.dot_general(left, right, (((0,), (0,)), ((), ())), preferred_element_...  145 us
    dot_general x7, matrix products, contract_last(): lax.dot_general(left, right, (((1,), (1,)), ((), ())), preferred_element_...  123 us
  transfers between devices with their start and end apart: 20, of which 12 were waited for; matrix products, arithmetic and copies ran while one was open for 12% of the time, Pallas kernels for 0%

commit v1 on v0

v1 whole, which is shorter than its diff:
```python
import functools
import math

import jax
import jax.numpy as jnp
from jax import lax
from jax.experimental import pallas as pl
from jax.experimental.pallas import tpu as pltpu
from jax.sharding import PartitionSpec as P
HEADS=32; KV_HEADS=8; HEAD_DIM=80; GROUP = HEADS // KV_HEADS
SPAN = KV_HEADS * HEAD_DIM
MIB = 1 << 20
epsilon = 1e-05
rope_base = 1000000.0
LOG2E=1.4426950408889634
SCALE=1.0/math.sqrt(HEAD_DIM)
NEG=-1e30
bf=jnp.bfloat16; f32=jnp.float32
LANES=128
UNROLL=8
WIDE=KV_HEADS*LANES

def nt(a, b):
    return lax.dot_general(a, b, (((1,), (1,)), ((), ())), preferred_element_type=f32)

def tn(a, b):
    return lax.dot_general(a, b, (((0,), (0,)), ((), ())), preferred_element_type=f32)

def nn(a, b):
    return jnp.dot(a, b, preferred_element_type=f32)

def picks(n_wide, span):
    row = lax.broadcasted_iota(jnp.int32, (n_wide, span), 0)
    col = lax.broadcasted_iota(jnp.int32, (n_wide, span), 1)
    head, d = row // LANES, row % LANES
    return jnp.where((col == head * HEAD_DIM + d) & (d < HEAD_DIM), 1.0, 0.0).astype(bf)

def fwd_kernel(Z, meta, q_ref, *refs):
    kv_refs = refs[:Z]
    sq_ref, sk_ref, o_ref, lse_ref, sel, q_s, k_s, vt_s, b_s, o_s = refs[Z:]
    seq = pl.program_id(0)
    L = q_ref.shape[1]
    span = KV_HEADS * HEAD_DIM
    mine = meta[0]
    steps = mine - meta[1 + seq] + 1

    @pl.when(seq == 0)
    def _():
        sel[...] = picks(WIDE, span)

    for c in range(GROUP):
        q_s[:, WIDE*c:WIDE*(c+1)] = nt(q_ref[0, :, span*c:span*(c+1)], sel[...]).astype(bf)
    seg_q = sq_ref[0]
    tri = lax.broadcasted_iota(jnp.int32, (L, L), 1) >= lax.broadcasted_iota(jnp.int32, (L, L), 0)
    ones_row = lax.broadcasted_iota(jnp.int32, (WIDE, L), 0) % LANES == HEAD_DIM
    for k in range(Z):
        @pl.when(k < steps)
        def _():
            k_s[k] = nt(kv_refs[k][0, :, :span], sel[...]).astype(bf)
            vt_s[k] = jnp.where(ones_row, 1.0, nt(sel[...], kv_refs[k][0, :, span:])).astype(bf)
            seg_k = sk_ref[0, pl.ds(pl.multiple_of((mine - k) * L, L), L), :]
            ok = seg_q == seg_k
            b_s[k] = jnp.where(ok & tri if k == 0 else ok, 0.0, NEG)
    def unit(u, _):
        hs = [u * UNROLL + i for i in range(UNROLL)]
        lanes = [pl.ds(pl.multiple_of((h // GROUP) * LANES, LANES), LANES) for h in hs]
        wides = [pl.ds(pl.multiple_of(h * LANES, LANES), LANES) for h in hs]
        def block(k, carry):
            bias = b_s[k]
            out = []
            for i in range(UNROLL):
                s = nt(k_s[k, :, lanes[i]], q_s[:, wides[i]]) + bias
                m = jnp.max(s, axis=0, keepdims=True)
                if carry is not None:
                    m = jnp.maximum(carry[i][0], m)
                p = jnp.exp2((s - m) * (SCALE * LOG2E)).astype(bf)
                o = nn(vt_s[k, lanes[i], :], p)
                if carry is not None:
                    o = carry[i][1] * jnp.exp2((carry[i][0] - m) * (SCALE * LOG2E)) + o
                out.append((m, o))
            return tuple(out)
        done = lax.fori_loop(1, steps, block, block(0, None))
        for i in range(UNROLL):
            m, acc = done[i]
            total = acc[HEAD_DIM:HEAD_DIM+1, :]
            o_s[wides[i], :] = (acc * (1.0 / total)).astype(bf)
            lse_ref[0, pl.ds(hs[i], 1), :] = m * (SCALE * LOG2E) + jnp.log2(total)
        return 0
    lax.fori_loop(0, HEADS // UNROLL, unit, 0)
    for c in range(GROUP):
        o_ref[0, :, span*c:span*(c+1)] = tn(o_s[WIDE*c:WIDE*(c+1), :], sel[...]).astype(bf)

def attend(meta, q, kvs, seg_q, seg_k):
    B, L, W = q.shape; Z = len(kvs); S = Z * L
    span = KV_HEADS * HEAD_DIM
    vm = pltpu.VMEM
    spec = lambda *s: pl.BlockSpec((1,) + s, lambda b, meta: (b,) + (0,) * len(s))
    return pl.pallas_call(
        functools.partial(fwd_kernel, Z),
        grid_spec=pltpu.PrefetchScalarGridSpec(
            num_scalar_prefetch=1, grid=(B,),
            in_specs=[spec(L, W)] + [spec(L, 2 * span)] * Z + [spec(1, L), spec(S, 1)],
            out_specs=[spec(L, W), spec(HEADS, L)],
            scratch_shapes=[vm((WIDE, span), bf), vm((L, HEADS * LANES), bf), vm((Z, L, WIDE), bf), vm((Z, WIDE, L), bf),
                            vm((Z, L, L), f32), vm((HEADS * LANES, L), bf)]),
        out_shape=[jax.ShapeDtypeStruct((B, L, W), bf), jax.ShapeDtypeStruct((B, HEADS, L), f32)],
        compiler_params=pltpu.CompilerParams(vmem_limit_bytes=56 << 20),
        name="attend_fwd",
    )(meta, q, *kvs, seg_q, seg_k)

def turn(x, cos, left, right):
    n = x.shape[1]
    return x * cos + pltpu.roll(x, n - HEAD_DIM // 2, 1) * left + pltpu.roll(x, HEAD_DIM // 2, 1) * right

def bwd_kernel(Z, meta, q_ref, *refs):
    kv_refs = refs[:Z]
    o_ref, do_ref, lse_ref, sq_ref, sk_ref, cq_ref, lq_ref, rq_ref, ck_ref, lk_ref, rk_ref = refs[Z:Z+11]
    dq_ref = refs[Z+11]; dkv_refs = refs[Z+12:2*Z+12]
    sel, q_s, d_s, k_s, kt_s, v_s, b_s, dqt_s, dk_s, dv_s, delta_s = refs[2*Z+12:]
    seq = pl.program_id(0)
    L = q_ref.shape[1]
    span = KV_HEADS * HEAD_DIM
    mine = meta[0]
    steps = mine - meta[1 + seq] + 1

    @pl.when(seq == 0)
    def _():
        sel[...] = picks(WIDE, span)

    head_row = lax.broadcasted_iota(jnp.int32, (KV_HEADS * 2, span), 0)
    column = lax.broadcasted_iota(jnp.int32, (KV_HEADS * 2, span), 1)
    heads = jnp.where(column // HEAD_DIM == head_row, 1.0, 0.0).astype(bf)
    for c in range(GROUP):
        cols = slice(span*c, span*(c+1)); wide = slice(WIDE*c, WIDE*(c+1))
        q_s[:, wide] = nt(q_ref[0, :, cols], sel[...]).astype(bf)
        d = do_ref[0, :, cols]
        d_s[:, wide] = nt(d, sel[...]).astype(bf)
        prod = o_ref[0, :, cols].astype(f32) * d.astype(f32)
        high = prod.astype(bf)
        rest = (prod - high.astype(f32)).astype(bf)
        delta_s[KV_HEADS*c:KV_HEADS*(c+1), :] = (nt(heads, high) + nt(heads, rest))[:KV_HEADS]
    seg_q = sq_ref[0]
    tri = lax.broadcasted_iota(jnp.int32, (L, L), 1) >= lax.broadcasted_iota(jnp.int32, (L, L), 0)
    for k in range(Z):
        @pl.when(k < steps)
        def _():
            k_s[k] = nt(kv_refs[k][0, :, :span], sel[...]).astype(bf)
            kt_s[k] = nt(sel[...], kv_refs[k][0, :, :span]).astype(bf)
            v_s[k] = nt(kv_refs[k][0, :, span:], sel[...]).astype(bf)
            seg_k = sk_ref[0, pl.ds(pl.multiple_of((mine - k) * L, L), L), :]
            ok = seg_q == seg_k
            b_s[k] = jnp.where(ok & tri if k == 0 else ok, 0.0, NEG)
    dqt_s[...] = jnp.zeros_like(dqt_s)
    def group(g, _):
        lanes = pl.ds(pl.multiple_of(g * LANES, LANES), LANES)
        def block(k, _):
            key = k_s[k, :, lanes]; value = v_s[k, :, lanes]; key_t = kt_s[k, lanes, :]
            bias = b_s[k]
            dk = jnp.zeros((L, LANES), f32); dv = jnp.zeros((L, LANES), f32)
            for i in range(GROUP):
                h = g * GROUP + i
                wide = pl.ds(pl.multiple_of(h * LANES, LANES), LANES)
                q = q_s[:, wide]; d = d_s[:, wide]
                p = jnp.exp2(nt(key, q) * (SCALE * LOG2E) + (bias - lse_ref[0, pl.ds(h, 1), :]))
                ds = (p * (nt(value, d) - delta_s[pl.ds(h, 1), :])).astype(bf)
                dv = dv + nn(p.astype(bf), d)
                dk = dk + nn(ds, q)
                dqt_s[wide, :] += nn(key_t, ds)
            dk_s[k, :, lanes] = (dk * SCALE).astype(bf)
            dv_s[k, :, lanes] = dv.astype(bf)
            return 0
        lax.fori_loop(0, steps, block, 0)
        return 0
    lax.fori_loop(0, KV_HEADS, group, 0)
    for c in range(GROUP):
        x = tn((dqt_s[WIDE*c:WIDE*(c+1), :] * SCALE).astype(bf), sel[...])
        dq_ref[0, :, span*c:span*(c+1)] = turn(x, cq_ref[...], lq_ref[...], rq_ref[...]).astype(bf)
    for k in range(Z):
        @pl.when(k < steps)
        def _():
            spot = pl.ds(pl.multiple_of((mine - k) * L, L), L)
            dkv_refs[k][0, :, :span] = turn(nn(dk_s[k], sel[...]), ck_ref[spot, :], lk_ref[spot, :], rk_ref[spot, :]).astype(bf)
            dkv_refs[k][0, :, span:] = nn(dv_s[k], sel[...]).astype(bf)
        @pl.when(k >= steps)
        def _():
            dkv_refs[k][...] = jnp.zeros_like(dkv_refs[k])

def attend_back(meta, q, kvs, o, do, lse, seg_q, seg_k, tab_q, tab_k):
    B, L, W = q.shape; Z = len(kvs); S = Z * L
    span = KV_HEADS * HEAD_DIM
    spec = lambda *s: pl.BlockSpec((1,) + s, lambda b, meta: (b,) + (0,) * len(s))
    fixed = lambda t: pl.BlockSpec(t.shape, lambda b, meta: (0, 0))
    vm = pltpu.VMEM
    return pl.pallas_call(
        functools.partial(bwd_kernel, Z),
        grid_spec=pltpu.PrefetchScalarGridSpec(
            num_scalar_prefetch=1, grid=(B,),
            in_specs=[spec(L, W)] + [spec(L, 2 * span)] * Z + [spec(L, W), spec(L, W), spec(HEADS, L), spec(1, L), spec(S, 1)]
              + [fixed(t) for t in tab_q + tab_k],
            out_specs=[spec(L, W)] + [spec(L, 2 * span)] * Z,
            scratch_shapes=[vm((WIDE, span), bf), vm((L, HEADS * LANES), bf), vm((L, HEADS * LANES), bf), vm((Z, L, WIDE), bf), vm((Z, WIDE, L), bf),
                            vm((Z, L, WIDE), bf), vm((Z, L, L), f32), vm((HEADS * LANES, L), f32), vm((Z, L, WIDE), bf), vm((Z, L, WIDE), bf), vm((HEADS, L), f32)]),
        out_shape=[jax.ShapeDtypeStruct((B, L, W), bf)] + [jax.ShapeDtypeStruct((B, L, 2 * span), bf)] * Z,
        compiler_params=pltpu.CompilerParams(vmem_limit_bytes=60 << 20),
        name="attend_bwd",
    )(meta, q, *kvs, o, do, lse, seg_q, seg_k, *tab_q, *tab_k)


def proj_kernel(turned, x_ref, w_ref, c_ref, l_ref, r_ref, y_ref):
    y = jnp.dot(x_ref[...], w_ref[...], preferred_element_type=f32)
    column = pl.program_id(0)

    @pl.when(column < turned)
    def _():
        y_ref[...] = turn(y, c_ref[...], l_ref[...], r_ref[...]).astype(bf)

    @pl.when(column >= turned)
    def _():
        y_ref[...] = y.astype(bf)


def project(x, w, tables, columns, turned):
    rows, width = x.shape
    length = tables[0].shape[0]
    return pl.pallas_call(
        functools.partial(proj_kernel, turned),
        grid=(columns, rows // length),
        in_specs=[
            pl.BlockSpec((length, width), lambda c, b: (b, 0)),
            pl.BlockSpec((width, SPAN), lambda c, b: (0, c)),
        ]
        + [pl.BlockSpec((length, SPAN), lambda c, b: (0, 0))] * 3,
        out_specs=pl.BlockSpec((length, SPAN), lambda c, b: (b, c)),
        out_shape=jax.ShapeDtypeStruct((rows, columns * SPAN), bf),
        compiler_params=pltpu.CompilerParams(vmem_limit_bytes=40 * MIB),
        cost_estimate=pl.CostEstimate(
            flops=2 * rows * width * columns * SPAN,
            bytes_accessed=2 * width * (rows + columns * SPAN),
            transcendentals=0,
        ),
        name="project",
    )(x, w, *tables)


def contract_last(left, right):
    return lax.dot_general(left, right, (((1,), (1,)), ((), ())), preferred_element_type=f32)


def contract_first(left, right):
    return lax.dot_general(left, right, (((0,), (0,)), ((), ())), preferred_element_type=f32)


def norm_back(grad_normed, unit, rstd, gain):
    scaled = grad_normed * gain
    return rstd * (scaled - unit * jnp.mean(scaled * unit, axis=-1, keepdims=True))


def gather(x, axis_name):
    return lax.all_gather(x, axis_name, axis=0, tiled=True)


def scatter(x, axis_name):
    return lax.psum_scatter(x, axis_name, scatter_dimension=0, tiled=True)


def right(x, count, axis_name="sp"):
    return lax.ppermute(x, axis_name, [(i, i + 1) for i in range(count)])


def left(x, count, parts, axis_name="sp"):
    return lax.ppermute(x, axis_name, [(i, i - 1) for i in range(parts - count, parts)])


def add(a, b):
    return a if b is None else (a.astype(f32) + b.astype(f32)).astype(bf)


def after(x, *others):
    others = [t for t in others if t is not None]
    return lax.optimization_barrier((x, *others))[0] if others else x


class Sum:
    def __init__(self, x, axis, parts, here):
        self.part = lambda c: lax.dynamic_index_in_dim(x, lax.rem(c + parts, parts), axis, keepdims=False)
        self.parts, self.here, self.step, self.up, self.down = parts, here, 1, None, None

    def go(self, *gates):
        if self.step >= self.parts:
            return ()
        up, down = self.up, self.down
        if up is not None:
            up, down = after(up, *gates), after(down, *gates)
        up = add(self.part(self.here + self.parts - self.step), up)
        down = add(self.part(self.here - self.parts + self.step), down)
        self.up, self.down = right(up, self.step), left(down, self.step, self.parts)
        self.step += 1
        return up, down

    def end(self, *gates):
        while self.step < self.parts:
            self.go()
        up, down = after(self.up, *gates), after(self.down, *gates)
        return (self.part(self.here).astype(f32) + up.astype(f32) + down.astype(f32)).astype(bf)


class Spread:
    def __init__(self, x, axis, parts, here, dtype, outs=1):
        self.x, self.axis, self.parts, self.here, self.dtype = x, axis, parts, here, dtype
        self.ups, self.downs = [x], [x]
        self.outs = outs

    def rise(self, *gates):
        step = len(self.ups)
        if step >= self.parts:
            return None
        send = after(self.ups[-1], *gates)
        self.ups.append(lax.ppermute(send, "sp", [(i, i + 1) for i in range(step - 1, self.parts - 1)]))
        return self.ups[-1]

    def fall(self, *gates):
        step = len(self.downs)
        if step >= self.parts:
            return None
        send = after(self.downs[-1], *gates)
        self.downs.append(lax.ppermute(send, "sp", [(i, i - 1) for i in range(1, self.parts - step + 1)]))
        return self.downs[-1]

    def go(self, *gates):
        self.rise(*gates)
        self.fall(*gates)

    def end(self):
        for _ in range(self.parts):
            self.go()
        pieces = [(self.here, self.x)]
        for step in range(1, self.parts):
            index = lax.rem(self.here - step + self.parts, self.parts)
            pieces.append((index, self.ups[step] + self.downs[self.parts - step]))
        whole = []
        for out in range(self.outs):
            choose = (lambda t: t) if self.outs == 1 else (lambda t: t[out])
            shape = choose(self.x).shape
            total = jnp.zeros(shape[: self.axis] + (self.parts,) + shape[self.axis :], self.dtype)
            for index, value in pieces:
                total = lax.dynamic_update_index_in_dim(total, choose(value).astype(self.dtype), index, self.axis)
            whole.append(total)
        return whole[0] if self.outs == 1 else whole


def split(x, parts):
    return x.reshape((parts, x.shape[0] // parts) + x.shape[1:])


def across(x, parts, here):
    shard = Sum(split(x, parts), 0, parts, here).end()
    return Spread(shard, 0, parts, here, f32).end().reshape(x.shape)


def tables_of(positions):
    half = HEAD_DIM // 2
    freqs = jnp.power(f32(rope_base), -jnp.arange(half, dtype=f32) * (2.0 / HEAD_DIM))
    angle = positions[:, None] * freqs[None, :]
    cosine, sine = jnp.cos(angle), jnp.sin(angle)
    none = jnp.zeros_like(sine)
    wide = lambda a, b: jnp.tile(jnp.concatenate([a, b], axis=1), (1, KV_HEADS))
    return wide(cosine, cosine), wide(sine, none), wide(none, sine)


def local(
    tokens, segments, w_query, w_key, w_value, w_out, w_gate, w_up, w_down, gain_attn, gain_mlp, cotangent
):
    seqs, length, width = tokens.shape
    seq_len = segments.shape[1]
    parts = lax.axis_size("sp")
    owners = lax.axis_size("fsdp")
    here = lax.axis_index("sp")
    rows = seqs * length
    ff = w_gate.shape[1]
    cols = ff // owners
    share = w_gate.shape[0] // parts

    own = lambda w: lax.dynamic_slice_in_dim(w, here * share, share, 0).astype(bf)
    pair = jnp.stack([own(w_gate), own(w_up)], axis=0).reshape(2 * share, ff)
    pair = lax.all_to_all(pair, "fsdp", split_axis=1, concat_axis=0, tiled=True)
    pair = pair.reshape(owners, 2, share, cols).transpose(0, 2, 1, 3).reshape(owners, share, 2 * cols)
    gains = jnp.pad(jnp.stack([gain_attn, gain_mlp], axis=1), ((0, 0), (0, 126)))
    kv_full = gather(jnp.concatenate([w_key.astype(bf), w_value.astype(bf), gains.astype(bf)], axis=1), "fsdp")
    gain_one = kv_full[:, 2 * SPAN].astype(f32)
    gain_two = kv_full[:, 2 * SPAN + 1].astype(f32)
    down = w_down.astype(bf)
    cot = cotangent.reshape(rows, width)

    cosine, sine_low, sine_high = tables_of(jnp.arange(seq_len, dtype=f32))
    mine = lambda t: lax.dynamic_slice_in_dim(t, here * length, length, 0)
    tab_own = (mine(cosine), mine(sine_low), mine(sine_high))
    tab_q = [tab_own[0], tab_own[1], -tab_own[2]]
    tab_k = [cosine, sine_low, -sine_high]
    tab_fwd = (tab_own[0], -tab_own[1], tab_own[2])

    seg_own = lax.dynamic_slice_in_dim(segments, here * length, length, 1)
    ends = segments.reshape(seqs, parts, length)[:, :, -1]
    first = jnp.sum((ends < seg_own[:, :1]).astype(jnp.int32), axis=1)
    meta = jnp.concatenate([here.astype(jnp.int32)[None], first])

    inputs = tokens.reshape(rows, width).astype(f32)
    rstd_one = lax.rsqrt(jnp.mean(inputs * inputs, axis=-1, keepdims=True) + epsilon)
    unit_one = inputs * rstd_one
    normed_one = after((unit_one * gain_one).astype(bf), pair)
    kv_own = project(normed_one, kv_full, tab_fwd, 2, 1).reshape(seqs, length, 2 * SPAN)
    query_full = gather(after(w_query.astype(bf), kv_own), "fsdp")
    kvs = [kv_own]
    for step in range(1, parts):
        kvs.append(lax.ppermute(kvs[-1], "sp", [(i, i + 1) for i in range(step - 1, parts - 1)]))
    query = project(normed_one, query_full, tab_fwd, HEADS // KV_HEADS, HEADS // KV_HEADS)
    ring = Spread(pair, 1, parts, here, bf)
    fallen = ring.fall()
    out_full = gather(after(w_out.astype(bf), query, kvs[-1], fallen), "fsdp")
    query = query.reshape(seqs, length, HEADS * HEAD_DIM)
    risen = ring.rise(kvs[-1])
    attn, logsum = attend(
        meta, query, kvs, seg_own[:, None, :], segments[:, :, None]
    )
    ring.fall()
    attn = after(attn, risen, ring.downs[-1])
    ring.rise(attn)
    attn_flat = attn.reshape(rows, HEADS * HEAD_DIM)
    resid = inputs + jnp.dot(attn_flat, out_full, preferred_element_type=f32)
    rstd_two = lax.rsqrt(jnp.mean(resid * resid, axis=-1, keepdims=True) + epsilon)
    unit_two = resid * rstd_two
    normed_two = (unit_two * gain_two).astype(bf)
    normed_all = gather(normed_two, "fsdp")
    cot_all = gather(after(cot, normed_two), "fsdp")
    ring.rise(normed_two)
    pair = ring.end().reshape(width, 2 * cols)

    both = jnp.dot(normed_all, pair, preferred_element_type=f32)
    grad_hidden = contract_last(cot_all, down)
    gate_pre, up_pre = both[:, :cols], both[:, cols:]
    sigma = jax.nn.sigmoid(gate_pre)
    silu_value = gate_pre * sigma
    hidden = (silu_value * up_pre).astype(bf)
    grad_gate = (grad_hidden * up_pre * sigma * (1.0 + gate_pre * (1.0 - sigma))).astype(bf)
    grad_up = (grad_hidden * silu_value).astype(bf)
    joined = lambda a, b: jnp.concatenate([a, b], axis=1)
    term_down = contract_first(hidden, cot_all).astype(bf)
    ring_down = Sum(split(term_down, parts), 0, parts, here)
    ring_down.go()
    grad_gate, grad_up = after(grad_gate, term_down), after(grad_up, term_down)
    grad_normed_two = contract_last(joined(grad_gate, grad_up), pair).astype(bf)
    sent = ring_down.go()
    grad_gate = after(grad_gate, grad_normed_two, *sent)
    grad_normed_two = scatter(after(grad_normed_two, *sent), "fsdp")
    rows_of = lambda t: t.reshape(owners, parts, share, cols)
    term_gate = contract_first(normed_all, grad_gate).astype(bf)
    ring_gate = Sum(rows_of(term_gate), 1, parts, here)
    grad_up = after(grad_up, *ring_gate.go(), *ring_down.go(term_gate))
    term_up = contract_first(normed_all, grad_up).astype(bf)
    ring_up = Sum(rows_of(term_up), 1, parts, here)
    hidden = after(hidden, *ring_up.go(), *ring_gate.go(term_up))
    grad_down = Spread(ring_down.end(), 0, parts, here, f32)
    grad_down.go()
    mlp_out = jnp.dot(after(hidden, grad_down.x), down, preferred_element_type=f32).astype(bf)
    sent = ring_gate.go() + ring_up.go()
    mlp_out = after(mlp_out, *sent)
    grad_down.go(mlp_out)
    shard_gate = ring_gate.end(mlp_out)
    grad_normed_two = after(grad_normed_two, mlp_out, shard_gate, *ring_up.go(mlp_out)).astype(f32)
    mlp_out = scatter(mlp_out, "fsdp")

    grad_resid = cot.astype(f32) + norm_back(grad_normed_two, unit_two, rstd_two, gain_two)
    grad_branch = grad_resid.astype(bf)
    grad_attn = contract_last(grad_branch, out_full).astype(bf)
    term_out = contract_first(attn_flat, after(grad_branch, grad_attn)).astype(bf)
    shard_pair = jnp.stack([shard_gate, ring_up.end()], axis=1)
    shard_pair = lax.all_to_all(shard_pair, "fsdp", split_axis=0, concat_axis=0, tiled=True)
    shard_pair = shard_pair.transpose(1, 2, 0, 3).reshape(2, share, ff)
    shard_out = scatter(after(term_out, shard_pair), "fsdp")
    grad_pair = Spread(shard_pair, 0, parts, here, f32, outs=2)
    grad_pair.go()
    grad_down.go(term_out)
    grad_attn = after(grad_attn, term_out, shard_pair).reshape(seqs, length, HEADS * HEAD_DIM)
    grad_query, passing = [], []
    for b in range(seqs):
        one = lambda t: t[b : b + 1]
        grad_q, *grad_kvs = attend_back(
            jnp.stack([meta[0], meta[1 + b]]), one(query), [one(t) for t in kvs], one(attn), one(grad_attn), one(logsum),
            seg_own[b : b + 1, None, :], segments[b : b + 1, :, None], tab_q, tab_k
        )
        grad_query.append(grad_q)
        passing.append([grad_kvs, None])
        gates = (grad_q,)
        if b < seqs - 1:
            grad_pair.go(*gates)
            grad_attn = after(grad_attn, grad_q, grad_pair.ups[1], grad_pair.downs[1])
    for step in range(1, parts):
        for b in range(seqs):
            grad_kvs, held = passing[b]
            passing[b][1] = left(add(grad_kvs[parts - step], held), step, parts)
        if step == 1:
            grad_query = jnp.concatenate(grad_query, axis=0).reshape(rows, HEADS * HEAD_DIM)
            term_query = contract_first(normed_one, grad_query).astype(bf)
            grad_pair.go(term_query)
            for held in passing:
                held[1] = after(held[1], term_query)
    shard_query = scatter(term_query, "fsdp")
    layer_out = (resid + after(mlp_out, term_query).astype(f32)).astype(bf)
    grad_kv = jnp.concatenate([add(grad_kvs[0], held) for grad_kvs, held in passing], axis=0)
    grad_kv = grad_kv.reshape(rows, 2 * SPAN)
    shard_kv = scatter(contract_first(normed_one, grad_kv).astype(bf), "fsdp")
    grad_normed_one = contract_last(grad_query, query_full) + contract_last(grad_kv, kv_full[:, : 2 * SPAN])
    grad_inputs = grad_resid + norm_back(grad_normed_one, unit_one, rstd_one, gain_one)
    grad_w_gate, grad_w_up = (t.reshape(parts * share, ff) for t in grad_pair.end())
    grad_down = grad_down.end().reshape(w_down.shape)
    shard_both = across(joined(shard_out, shard_query), parts, here)
    shard_out, shard_query = shard_both[:, :width], shard_both[:, width:]
    shard_kv = lax.psum(shard_kv, "sp").astype(f32)
    grad_key, grad_value = shard_kv[:, :SPAN], shard_kv[:, SPAN:]
    along = lambda w, g: jnp.sum(w.astype(bf).astype(f32) * g, axis=1)
    low_gain = lambda gain: gain.astype(bf).astype(f32)
    grad_gain_attn = along(w_query, shard_query) + along(w_key, grad_key) + along(w_value, grad_value)
    grad_gain_mlp = along(w_gate, grad_w_gate) + along(w_up, grad_w_up)
    return (
        layer_out.reshape(seqs, length, width),
        grad_inputs.reshape(seqs, length, width),
        shard_query,
        grad_key,
        grad_value,
        shard_out,
        grad_w_gate,
        grad_w_up,
        grad_down,
        grad_gain_attn / low_gain(gain_attn),
        grad_gain_mlp / low_gain(gain_mlp),
    )


def solution(mesh):
    data, rows, lone = P("fsdp", "sp", None), P("fsdp", None), P("fsdp")
    return jax.shard_map(
        local,
        mesh=mesh,
        in_specs=(data, rows) + (rows,) * 7 + (lone, lone, data),
        out_specs=(data, data) + (rows,) * 7 + (lone, lone),
        check_vma=False,
    )
```

time: 4150 us -> 1530 us (0.37)
  waiting for transfers between devices: 3030 us -> 626 us
  matrix products: 580 us -> 324 us
  blocking collectives: 185 us -> 31.6 us
  starting transfers between devices: 25.1 us -> 148 us
  Pallas kernels: 0 us -> 114 us
  local copies, waits for them, and re-layouts: 173 us -> 103 us
    reduce_scatter x7 -> x5, waiting for transfers between devices: 1440 us -> 26.7 us  [scatter(): return lax.psum_scatter(x, axis_name, scatter_dimension=0, tiled=True)]
    psum x1, waiting for transfers between devices: 1090 us -> 40 us  [local(): shard_kv = lax.psum(shard_kv, 'sp').astype(f32)]
    ppermute x0 -> x57, waiting for transfers between devices: none -> 332 us  [the longest x12 108 us: fall(): lax.ppermute(send, 'sp', [(i, i - 1) for i in range(1, self.parts - step...]
    dot_general x35 -> x3, matrix products: 312 us -> 98.1 us  [the longest x1 46.7 us: local(): both = jnp.dot(normed_all, pair, preferred_element_type=f32)]
    all_to_all x5 -> x1, waiting for transfers between devices: 168 us -> 20.8 us  [local(): pair = lax.all_to_all(pair, 'fsdp', split_axis=1, concat_axis=0, tiled=True)]
    ppermute x0 -> x57, starting transfers between devices: none -> 142 us  [the longest x12 56.7 us: right(): return lax.ppermute(x, axis_name, [(i, i + 1) for i in range(count)])]
    all_gather x7 -> x5, waiting for transfers between devices: 328 us -> 205 us  [gather(): return lax.all_gather(x, axis_name, axis=0, tiled=True)]
    pallas_call x0 -> x5, Pallas kernels: none -> 114 us  [the longest x2 55.3 us: attend_back(): pl.pallas_call(functools.partial(bwd_kernel, Z), grid_spec=pltpu.Prefetch...]
  transfers between devices with their start and end apart: 20 -> 69, of which waited for: 12 -> 32; matrix products, arithmetic and copies ran while one was open for 12% -> 27% of each run, Pallas kernels for 0% -> 7%
where the time goes in v1:
time: 1530 us; the launch traced here: 1510 us
  waiting for transfers between devices  626 us (41%)
  matrix products  324 us (21%)
  other arithmetic  151 us (10%)
  starting transfers between devices  148 us (10%)
  Pallas kernels  114 us (7%)
  local copies, waits for them, and re-layouts  103 us (7%)
  blocking collectives  31.6 us (2%)
  between operations  15.8 us (1%)
    all_gather x5, waiting for transfers between devices, gather(): return lax.all_gather(x, axis_name, axis=0, tiled=True)  205 us
    dot_general x5, matrix products, contract_last(): lax.dot_general(left, right, (((1,), (1,)), ((), ())), preferred_element_...  120 us
    ppermute x12, waiting for transfers between devices, fall(): lax.ppermute(send, 'sp', [(i, i - 1) for i in range(1, self.parts - step...  108 us
    dot_general x6, matrix products, contract_first(): lax.dot_general(left, right, (((0,), (0,)), ((), ())), preferred_element_...  107 us
    ppermute x18, waiting for transfers between devices, left(): lax.ppermute(x, axis_name, [(i, i - 1) for i in range(parts - count, part...  89.2 us
    ppermute x12, waiting for transfers between devices, right(): return lax.ppermute(x, axis_name, [(i, i + 1) for i in range(count)])  70.1 us
    ppermute x12, starting transfers between devices, right(): return lax.ppermute(x, axis_name, [(i, i + 1) for i in range(count)])  56.7 us
    pallas_call x2, Pallas kernels, attend_back(): pl.pallas_call(functools.partial(bwd_kernel, Z), grid_spec=pltpu.Prefetch...  55.3 us
  transfers between devices with their start and end apart: 69, of which 32 were waited for; matrix products, arithmetic and copies ran while one was open for 27% of the time, Pallas kernels for 7%

profile of v1, /device:TPU:0, one launch (start us, length us, event | category | flops | bytes accessed | tf_op | source)
XLA Modules:
  0.0 1513.3 jit_solution(16239049731154584556)
XLA Ops:
  39.8 20.8 %all-to-all-done = bf16[160,8,896]{2,0,1:T(8,128)(2,1)} async-done(((bf16[160,8,896]{2,0,1:T(8,128)(2,1)}), bf16[160,8,896]{2,0,1:T(8,128)(2,1)}, u32[]{:S(2)}, u32[]{:S(2)}) %all-to-all-start) | async-done | bytes 2293792 | tf_op jit(solution)/shard_map/all_to_all | solution.py:385
  64.0 22.3 %all-gather.6.cloned.1.call-done.w_ref = bf16[2560,1408]{1,0:T(8,128)(2,1)} async-done(((bf16[320,1408]{1,0:T(8,128)(2,1)}), bf16[2560,1408]{1,0:T(8,128)(2,1)}) %all-gather.6.cloned.1.call-update) | async-done | bytes 7208976 | tf_op jit(solution)/shard_map/all_gather | solution.py:259
  105.1 28.4 %collective-permute-done.refs_1_ = bf16[2,256,1280]{2,1,0:T(8,128)(2,1)S(1)} collective-permute-done((bf16[2,256,1280]{2,1,0:T(8,128)(2,1)S(1)}, bf16[2,256,1280]{2,1,0:T(8,128)(2,1)S(1)}, u32[]{:S(2)}, u32[]{:S(2)}) %collective-permute-start) | collective-permute-done | bytes 1310752 | tf_op jit(solution)/shard_map/ppermute | solution.py:414
  142.6 33.5 %all-gather.8.cloned.1.call-done.w_ref = bf16[2560,2560]{1,0:T(8,128)(2,1)} async-done(((bf16[320,2560]{1,0:T(8,128)(2,1)}), bf16[2560,2560]{1,0:T(8,128)(2,1)}) %all-gather.8.cloned.1.call-update) | async-done | bytes 13107216 | tf_op jit(solution)/shard_map/all_gather | solution.py:259
  206.4 35.2 %attend_fwd.1 = (bf16[2,256,2560]{2,1,0:T(8,128)(2,1)}, f32[2,32,256]{2,1,0:T(8,128)}) custom-call(s32[3]{0:T(128)} %pad_add_fusion.meta, bf16[2,256,2560]{2,1,0:T(8,128)(2,1)} %bitcast.258, bf16[2,256,1280]{2,1,0:T(8,128)(2,1)} %bitcast.257, bf16[2,256,1280]{2,1,0:T(8,128)(2,1)} %copy-done.33, bf16[2,256,1280]{2,1,0:T(8,128)(2,1)} %collective-permute-done.1.refs_2_, ...), custom_call_target="tpu_custom_call" | custom-call | tf_op jit(solution)/shard_map/attend_fwd/pallas_call | solution.py:98
  251.2 22.4 %all-gather.10.cloned.1.call-done = bf16[2560,2560]{1,0:T(8,128)(2,1)} async-done(((bf16[320,2560]{1,0:T(8,128)(2,1)}), bf16[2560,2560]{1,0:T(8,128)(2,1)}) %all-gather.10.cloned.1.call-update) | async-done | bytes 13107216 | tf_op jit(solution)/shard_map/all_gather | solution.py:259
  273.6 21.7 %multiply_reduce_fusion.3 = (f32[512]{0:T(512)S(1)}, f32[512,2560]{1,0:T(8,128)S(1)}) fusion(bf16[512,2560]{1,0:T(8,128)(2,1)} %bitcast.300, bf16[2560,2560]{1,0:T(8,128)(2,1)} %all-gather.10.cloned.1.call-done, bf16[2,256,2560]{2,1,0:T(8,128)(2,1)S(1)} %copy-done.20), kind=kOutput, calls=%fused_computation.38 | convolution fusion | flops 6716128768 | bytes 23595008 | tf_op jit(solution)/shard_map/dot_general | solution.py:428
  321.8 33.1 %collective-permute-done.6 = bf16[8,80,1792]{2,1,0:T(8,128)(2,1)} collective-permute-done((bf16[8,80,1792]{2,1,0:T(8,128)(2,1)}, bf16[8,80,1792]{2,1,0:T(8,128)(2,1)}, u32[]{:S(2)}, u32[]{:S(2)}) %collective-permute-start.6) | collective-permute-done | bytes 2293792 | tf_op jit(solution)/shard_map/ppermute | solution.py:326
  367.6 64.0 %all-gather.12.cloned.1.call-done = bf16[4096,2560]{1,0:T(8,128)(2,1)} async-done(((bf16[512,2560]{1,0:T(8,128)(2,1)}), bf16[4096,2560]{1,0:T(8,128)(2,1)}) %all-gather.12.cloned.1.call-update) | async-done | bytes 20971536 | tf_op jit(solution)/shard_map/all_gather | solution.py:259
  431.6 46.7 %fusion.67 = f32[4096,1792]{1,0:T(8,128)} fusion(bf16[4096,2560]{1,0:T(8,128)(2,1)} %all-gather.12.cloned.1.call-done, bf16[2560,1792]{1,0:T(8,128)(2,1)} %bitcast.24), kind=kOutput, calls=%fused_computation.185 | convolution fusion | flops 37580963840 | bytes 59506688 | tf_op jit(solution)/shard_map/dot_general | solution.py:437
  478.3 62.7 %all-gather.14.cloned.1.call-done = bf16[4096,2560]{1,0:T(8,128)(2,1)} async-done(((bf16[512,2560]{1,0:T(8,128)(2,1)}), bf16[4096,2560]{1,0:T(8,128)(2,1)}) %all-gather.14.cloned.1.call-update) | async-done | bytes 20971536 | tf_op jit(solution)/shard_map/all_gather | solution.py:259
  541.0 38.0 %multiply_convert_fusion = (bf16[4096,896]{1,0:T(8,128)(2,1)}, bf16[4096,896]{1,0:T(8,128)(2,1)}, bf16[4096,896]{1,0:T(8,128)(2,1)}) fusion(f32[4096,1792]{1,0:T(8,128)} %fusion.67, bf16[4096,2560]{1,0:T(8,128)(2,1)} %all-gather.14.cloned.1.call-done, f32[896,2560]{1,0:T(8,128)} %param.20), kind=kOutput, calls=%fused_computation.7 | convolution fusion | flops 18847825920 | bytes 81526784 | tf_op jit(solution)/shard_map/dot_general | solution.py:246
  578.9 24.5 %convolution_convert_fusion.7 = bf16[896,2560]{1,0:T(8,128)(2,1)S(1)} fusion(bf16[4096,896]{1,0:T(8,128)(2,1)} %get-tuple-element.81, bf16[4096,2560]{1,0:T(8,128)(2,1)} %all-gather.14.cloned.1.call-done), kind=kOutput, calls=%fused_computation.19 | convolution fusion | flops 18792775680 | bytes 32899072 | tf_op jit(solution)/shard_map/dot_general | solution.py:250
  610.8 46.6 %convolution_convert_fusion = bf16[4096,2560]{1,0:T(8,128)(2,1)} fusion(bf16[2560,1792]{1,0:T(8,128)(2,1)} %bitcast.24, bf16[4096,896]{1,0:T(8,128)(2,1)S(1)} %copy-done.69, bf16[4096,896]{1,0:T(8,128)(2,1)} %get-tuple-element.74), kind=kOutput, calls=%fused_computation | convolution fusion | flops 37620809728 | bytes 44826624 | tf_op jit(solution)/shard_map/dot_general | solution.py:246
  663.7 29.0 %convolution_convert_fusion.6 = bf16[2560,896]{1,0:T(8,128)(2,1)S(1)} fusion(bf16[4096,2560]{1,0:T(8,128)(2,1)} %all-gather.12.cloned.1.call-done, bf16[4096,896]{1,0:T(8,128)(2,1)} %get-tuple-element.74), kind=kOutput, calls=%fused_computation.18 | convolution fusion | flops 18792775680 | bytes 32899072 | tf_op jit(solution)/shard_map/dot_general | solution.py:250
  701.5 27.2 %convolution_convert_fusion.5 = bf16[2560,896]{1,0:T(8,128)(2,1)S(1)} fusion(bf16[4096,2560]{1,0:T(8,128)(2,1)} %all-gather.12.cloned.1.call-done, bf16[4096,896]{1,0:T(8,128)(2,1)} %get-tuple-element.77), kind=kOutput, calls=%fused_computation.17 | convolution fusion | flops 18792775680 | bytes 32899072 | tf_op jit(solution)/shard_map/dot_general | solution.py:250
  793.9 29.7 %convolution_convert_fusion.1 = bf16[4096,2560]{1,0:T(8,128)(2,1)} fusion(bf16[4096,896]{1,0:T(8,128)(2,1)} %get-tuple-element.81, f32[896,2560]{1,0:T(8,128)} %param.20), kind=kOutput, calls=%fused_computation.1 | convolution fusion | flops 18803261440 | bytes 37486592 | tf_op jit(solution)/shard_map/dot_general | solution.py:463
  887.7 31.6 %all_to_all.21 = bf16[8,2,80,896]{3,2,1,0:T(8,128)(2,1)S(1)} all-to-all(bf16[8,2,80,896]{3,2,1,0:T(8,128)(2,1)S(1)} %pad_maximum_fusion.3), channel_id=1, replica_groups=mesh['fsdp'=8,'sp'=4] {'fsdp'}, dimensions={0} | all-to-all | bytes 4587520 | tf_op jit(solution)/shard_map/all_to_all | solution.py:476
  982.6 27.4 %attend_bwd.2 = (bf16[1,256,2560]{2,1,0:T(8,128)(2,1)}, bf16[1,256,1280]{2,1,0:T(8,128)(2,1)}, bf16[1,256,1280]{2,1,0:T(8,128)(2,1)}, bf16[1,256,1280]{2,1,0:T(8,128)(2,1)}, bf16[1,256,1280]{2,1,0:T(8,128)(2,1)}) custom-call(s32[2]{0:T(128)} %get-tuple-element.197.meta, bf16[1,256,2560]{2,1,0:T(8,128)(2,1)} %get-tuple-element.161.q_ref, ...), custom_call_target="tpu_custom_call" | custom-call | tf_op jit(solution)/shard_map/attend_bwd/pallas_call | solution.py:194
  1030.0 27.9 %attend_bwd.3 = (bf16[1,256,2560]{2,1,0:T(8,128)(2,1)}, bf16[1,256,1280]{2,1,0:T(8,128)(2,1)}, bf16[1,256,1280]{2,1,0:T(8,128)(2,1)}, bf16[1,256,1280]{2,1,0:T(8,128)(2,1)}, bf16[1,256,1280]{2,1,0:T(8,128)(2,1)}) custom-call(s32[2]{0:T(128)} %get-tuple-element.198.meta, bf16[1,256,2560]{2,1,0:T(8,128)(2,1)} %get-tuple-element.162.q_ref, ...), custom_call_target="tpu_custom_call" | custom-call | tf_op jit(solution)/shard_map/attend_bwd/pallas_call | solution.py:194
  1087.6 21.8 %collective-permute-done.51 = bf16[224,2560]{1,0:T(8,128)(2,1)S(1)} collective-permute-done((bf16[224,2560]{1,0:T(8,128)(2,1)}, bf16[224,2560]{1,0:T(8,128)(2,1)S(1)}, u32[]{:S(2)}, u32[]{:S(2)}) %collective-permute-start.51) | collective-permute-done | bytes 1146912 | tf_op jit(solution)/shard_map/ppermute | solution.py:318
  1197.3 56.0 %collective-permute-done.31 = bf16[1,256,1280]{2,1,0:T(8,128)(2,1)S(1)} collective-permute-done((bf16[1,256,1280]{2,1,0:T(8,128)(2,1)S(1)}, bf16[1,256,1280]{2,1,0:T(8,128)(2,1)S(1)}, u32[]{:S(2)}, u32[]{:S(2)}) %collective-permute-start.31) | collective-permute-done | bytes 655392 | tf_op jit(solution)/shard_map/ppermute | solution.py:271
  1317.8 26.7 %reduce-scatter.6.cloned.1.call-done = bf16[512,2560]{1,0:T(8,128)(2,1)} async-done(((bf16[4096,2560]{1,0:T(8,128)(2,1)}), bf16[512,2560]{1,0:T(8,128)(2,1)}) %reduce-scatter.6.cloned.1.call-update) | async-done | bytes 2621456 | tf_op jit(solution)/shard_map/reduce_scatter | solution.py:263
  1448.6 40.0 %all-reduce.5.cloned.1.call-done = bf16[320,1280]{1,0:T(8,128)(2,1)} async-done(((bf16[320,1280]{1,0:T(8,128)(2,1)}), bf16[320,1280]{1,0:T(8,128)(2,1)}) %all-reduce.5.cloned.1.call-update) | async-done | bytes 819216 | tf_op jit(solution)/shard_map/psum | solution.py:517
  (431 shorter events, 680.5 us)
Async XLA Ops:
  7.2 79.1 %all-gather.6.cloned.1.call-start = ((), (), s32[]{:S(2)}) async-start(), calls=%async_computation.7 | async-start | bytes 8110080 | tf_op jit(solution)/shard_map/all_gather | solution.py:259
  22.6 153.5 %all-gather.8.cloned.1.call-start = ((), (), s32[]{:S(2)}) async-start(), calls=%async_computation.8 | async-start | bytes 14745600 | tf_op jit(solution)/shard_map/all_gather | solution.py:259
  101.6 172.0 %all-gather.10.cloned.1.call-start = ((), (), s32[]{:S(2)}) async-start(), calls=%async_computation.9 | async-start | bytes 14745600 | tf_op jit(solution)/shard_map/all_gather | solution.py:259
  136.3 59.4 %collective-permute-start.4 = (bf16[8,80,1792]{2,1,0:T(8,128)(2,1)}, bf16[8,80,1792]{2,1,0:T(8,128)(2,1)}, u32[]{:S(2)}, u32[]{:S(2)}) collective-permute-start(bf16[8,80,1792]{2,1,0:T(8,128)(2,1)} %bitcast.305), channel_id=1, source_target_pairs={{1,0},{2,1},{3,2},{5,4},{6,5},{7,6},{9,8},{10,9},{11,10},{13,12},{... | collective-permute-start | bytes 6881288 | tf_op jit(solution)/shard_map/ppermute | solution.py:326
  137.6 58.1 %collective-permute-start.2 = (bf16[2,256,1280]{2,1,0:T(8,128)(2,1)}, bf16[2,256,1280]{2,1,0:T(8,128)(2,1)}, u32[]{:S(2)}, u32[]{:S(2)}) collective-permute-start(bf16[2,256,1280]{2,1,0:T(8,128)(2,1)} %collective-permute-done.1.refs_2_), channel_id=1, source_target_pairs={{2,3},{6,7},{10,11},{14,15},{18,19},{22,23},{26,27},{30,31}} | collective-permute-start | bytes 3932168 | tf_op jit(solution)/shard_map/ppermute | solution.py:414
  195.8 235.8 %all-gather.12.cloned.1.call-start = ((), (), s32[]{:S(2)}) async-start(), calls=%async_computation.10 | async-start | bytes 23592960 | tf_op jit(solution)/shard_map/all_gather | solution.py:259
  299.7 241.3 %all-gather.14.cloned.1.call-start = ((), (), s32[]{:S(2)}) async-start(), calls=%async_computation.11 | async-start | bytes 23592960 | tf_op jit(solution)/shard_map/all_gather | solution.py:259
  300.3 622.1 %reduce-scatter.8.cloned.1.call-start = ((), (), s32[]{:S(2)}) async-start(), calls=%async_computation.13 | async-start | bytes 23592960 | tf_op jit(solution)/shard_map/reduce_scatter | solution.py:263
  303.7 59.7 %collective-permute-start.8 = (bf16[8,80,1792]{2,1,0:T(8,128)(2,1)}, bf16[8,80,1792]{2,1,0:T(8,128)(2,1)}, u32[]{:S(2)}, u32[]{:S(2)}) collective-permute-start(bf16[8,80,1792]{2,1,0:T(8,128)(2,1)} %collective-permute-done.7), channel_id=1, source_target_pairs={{2,3},{6,7},{10,11},{14,15},{18,19},{22,23},{26,27},{30,31}} | collective-permute-start | bytes 6881288 | tf_op jit(solution)/shard_map/ppermute | solution.py:318
  661.3 607.1 %reduce-scatter.10.cloned.1.call-start = ((), (), s32[]{:S(2)}) async-start(), calls=%async_computation.14 | async-start | bytes 14745600 | tf_op jit(solution)/shard_map/reduce_scatter | solution.py:263
  744.7 78.9 %collective-permute-start.17 = (bf16[8,80,896]{2,1,0:T(8,128)(2,1)}, bf16[8,80,896]{2,1,0:T(8,128)(2,1)}, u32[]{:S(2)}, u32[]{:S(2)}) collective-permute-start(bf16[8,80,896]{2,1,0:T(8,128)(2,1)} %get-tuple-element.144), channel_id=1, source_target_pairs={{0,1},{1,2},{4,5},{5,6},{8,9},{9,10},{12,13},{13,14},{16,17},{17,1... | collective-permute-start | bytes 3440648 | tf_op jit(solution)/shard_map/ppermute | solution.py:267
  759.7 63.9 %collective-permute-start.18 = (bf16[8,80,896]{2,1,0:T(8,128)(2,1)}, bf16[8,80,896]{2,1,0:T(8,128)(2,1)}, u32[]{:S(2)}, u32[]{:S(2)}) collective-permute-start(bf16[8,80,896]{2,1,0:T(8,128)(2,1)} %get-tuple-element.143), channel_id=1, source_target_pairs={{2,1},{3,2},{6,5},{7,6},{10,9},{11,10},{14,13},{15,14},{18,17},{19... | collective-permute-start | bytes 3440648 | tf_op jit(solution)/shard_map/ppermute | solution.py:271
  765.1 68.3 %collective-permute-start.23 = (bf16[8,80,896]{2,1,0:T(8,128)(2,1)}, bf16[8,80,896]{2,1,0:T(8,128)(2,1)}, u32[]{:S(2)}, u32[]{:S(2)}) collective-permute-start(bf16[8,80,896]{2,1,0:T(8,128)(2,1)} %get-tuple-element.140), channel_id=1, source_target_pairs={{0,1},{1,2},{4,5},{5,6},{8,9},{9,10},{12,13},{13,14},{16,17},{17,1... | collective-permute-start | bytes 3440648 | tf_op jit(solution)/shard_map/ppermute | solution.py:267
  953.0 315.4 %reduce-scatter.12.cloned.1.call-start = ((), (), s32[]{:S(2)}) async-start(), calls=%async_computation.15 | async-start | bytes 14745600 | tf_op jit(solution)/shard_map/reduce_scatter | solution.py:263
  1071.6 272.9 %reduce-scatter.6.cloned.1.call-start = ((), (), s32[]{:S(2)}) async-start(), calls=%async_computation.12 | async-start | bytes 23592960 | tf_op jit(solution)/shard_map/reduce_scatter | solution.py:263
  1072.4 361.2 %reduce-scatter.14.cloned.1.call-start = ((), (), s32[]{:S(2)}) async-start(), calls=%async_computation.16 | async-start | bytes 7372800 | tf_op jit(solution)/shard_map/reduce_scatter | solution.py:263
  1109.5 61.8 %collective-permute-start.55 = (bf16[224,2560]{1,0:T(8,128)(2,1)S(1)}, bf16[224,2560]{1,0:T(8,128)(2,1)S(1)}, u32[]{:S(2)}, u32[]{:S(2)}) collective-permute-start(bf16[224,2560]{1,0:T(8,128)(2,1)S(1)} %collective-permute-done.51), channel_id=1, source_target_pairs={{1,2},{2,3},{5,6},{6,7},{9,10},{10,11},{13,14},{14,15},{17,18},{18... | collective-permute-start | bytes 3440648 | tf_op jit(solution)/shard_map/ppermute | solution.py:318
  1131.6 182.8 %collective-permute-start.49 = (bf16[2,80,7168]{2,1,0:T(8,128)(2,1)}, bf16[2,80,7168]{2,1,0:T(8,128)(2,1)}, u32[]{:S(2)}, u32[]{:S(2)}) collective-permute-start(bf16[2,80,7168]{2,1,0:T(8,128)(2,1)} %collective-permute-done.27), channel_id=1, source_target_pairs={{1,2},{2,3},{5,6},{6,7},{9,10},{10,11},{13,14},{14,15},{17,18},{18... | collective-permute-start | bytes 6881288 | tf_op jit(solution)/shard_map/ppermute | solution.py:318
  1171.3 145.2 %collective-permute-start.47 = (bf16[2,80,7168]{2,1,0:T(8,128)(2,1)}, bf16[2,80,7168]{2,1,0:T(8,128)(2,1)}, u32[]{:S(2)}, u32[]{:S(2)}) collective-permute-start(bf16[2,80,7168]{2,1,0:T(8,128)(2,1)} %collective-permute-done.28), channel_id=1, source_target_pairs={{1,0},{2,1},{5,4},{6,5},{9,8},{10,9},{13,12},{14,13},{17,16},{18,1... | collective-permute-start | bytes 6881288 | tf_op jit(solution)/shard_map/ppermute | solution.py:326
  1192.4 60.8 %collective-permute-start.31 = (bf16[1,256,1280]{2,1,0:T(8,128)(2,1)S(1)}, bf16[1,256,1280]{2,1,0:T(8,128)(2,1)S(1)}, u32[]{:S(2)}, u32[]{:S(2)}) collective-permute-start(bf16[1,256,1280]{2,1,0:T(8,128)(2,1)S(1)} %add_convert_fusion.5), channel_id=1, source_target_pairs={{1,0},{2,1},{3,2},{5,4},{6,5},{7,6},{9,8},{10,9},{11,10},{13,12},{... | collective-permute-start | bytes 1966088 | tf_op jit(solution)/shard_map/ppermute | solution.py:271
  1194.1 73.3 %collective-permute-start.34 = (bf16[1,256,1280]{2,1,0:T(8,128)(2,1)S(1)}, bf16[1,256,1280]{2,1,0:T(8,128)(2,1)S(1)}, u32[]{:S(2)}, u32[]{:S(2)}) collective-permute-start(bf16[1,256,1280]{2,1,0:T(8,128)(2,1)S(1)} %add_convert_fusion.2), channel_id=1, source_target_pairs={{1,0},{2,1},{3,2},{5,4},{6,5},{7,6},{9,8},{10,9},{11,10},{13,12},{... | collective-permute-start | bytes 1966088 | tf_op jit(solution)/shard_map/ppermute | solution.py:271
  1288.3 200.3 %all-reduce.5.cloned.1.call-start = ((), (), s32[]{:S(2)}) async-start(), calls=%async_computation.17 | async-start | bytes 1638400 | tf_op jit(solution)/shard_map/psum | solution.py:517
  1288.4 60.7 %collective-permute-start.38 = (bf16[80,5120]{1,0:T(8,128)(2,1)}, bf16[80,5120]{1,0:T(8,128)(2,1)}, u32[]{:S(2)}, u32[]{:S(2)}) collective-permute-start(bf16[80,5120]{1,0:T(8,128)(2,1)} %get-tuple-element.158), channel_id=1, source_target_pairs={{3,2},{7,6},{11,10},{15,14},{19,18},{23,22},{27,26},{31,30}} | collective-permute-start | bytes 2457608 | tf_op jit(solution)/shard_map/ppermute | solution.py:271
  1314.4 87.3 %collective-permute-start.50 = (bf16[2,80,7168]{2,1,0:T(8,128)(2,1)}, bf16[2,80,7168]{2,1,0:T(8,128)(2,1)}, u32[]{:S(2)}, u32[]{:S(2)}) collective-permute-start(bf16[2,80,7168]{2,1,0:T(8,128)(2,1)} %collective-permute-done.49), channel_id=1, source_target_pairs={{2,3},{6,7},{10,11},{14,15},{18,19},{22,23},{26,27},{30,31}} | collective-permute-start | bytes 6881288 | tf_op jit(solution)/shard_map/ppermute | solution.py:318
  (123 other events, 3026.9 us)
Sparse Core Ops, SparseCore 0:
  12.3 73.9 all-gather.5
  101.7 74.3 all-gather.7
  195.9 77.6 all-gather.9
  299.8 131.7 all-gather.11
  433.3 107.5 all-gather.13
  661.4 134.9 reduce-scatter.7
  953.1 93.8 reduce-scatter.9
  1071.7 133.1 reduce-scatter.11
  1208.5 135.9 reduce-scatter.5
  1347.8 63.0 reduce-scatter.13
  1433.8 54.8 all-reduce.4

commit v2 on v1

--- a/solution.py
+++ b/solution.py
@@ -462,11 +462,11 @@
     grad_down.go()
     mlp_out = jnp.dot(after(hidden, grad_down.x), down, preferred_element_type=f32).astype(bf)
     sent = ring_gate.go() + ring_up.go()
-    mlp_out = after(mlp_out, *sent)
-    grad_down.go(mlp_out)
-    shard_gate = ring_gate.end(mlp_out)
-    grad_normed_two = after(grad_normed_two, mlp_out, shard_gate, *ring_up.go(mlp_out)).astype(f32)
+    ready = after(mlp_out, *sent)
     mlp_out = scatter(mlp_out, "fsdp")
+    grad_down.go(ready)
+    shard_gate = ring_gate.end(ready)
+    grad_normed_two = after(grad_normed_two, ready, shard_gate, *ring_up.go(ready)).astype(f32)
 
     grad_resid = cot.astype(f32) + norm_back(grad_normed_two, unit_two, rstd_two, gain_two)
     grad_branch = grad_resid.astype(bf)
@@ -475,7 +475,7 @@
     shard_pair = jnp.stack([shard_gate, ring_up.end()], axis=1)
     shard_pair = lax.all_to_all(shard_pair, "fsdp", split_axis=0, concat_axis=0, tiled=True)
     shard_pair = shard_pair.transpose(1, 2, 0, 3).reshape(2, share, ff)
-    shard_out = scatter(after(term_out, shard_pair), "fsdp")
+    shard_out = scatter(term_out, "fsdp")
     grad_pair = Spread(shard_pair, 0, parts, here, f32, outs=2)
     grad_pair.go()
     grad_down.go(term_out)

time: 1530 us -> 1610 us (1.052)
  waiting for transfers between devices: 626 us -> 719 us
  blocking collectives: 31.6 us -> 0 us
    reduce_scatter x5, waiting for transfers between devices: 26.7 us -> 130 us  [scatter(): return lax.psum_scatter(x, axis_name, scatter_dimension=0, tiled=True)]
    all_to_all x1 -> x0, blocking collectives: 31.6 us -> none  [local(): lax.all_to_all(shard_pair, 'fsdp', split_axis=0, concat_axis=0, tiled=True)]
    all_to_all x0 -> x1, waiting for transfers between devices: none -> 21 us  [local(): lax.all_to_all(shard_pair, 'fsdp', split_axis=0, concat_axis=0, tiled=True)]
    unnamed x159 -> x157, local copies, waits for them, and re-layouts: 35.9 us -> 34.2 us
  transfers between devices with their start and end apart: 69 -> 70, of which waited for: 32 -> 32; matrix products, arithmetic and copies ran while one was open for 27% -> 27% of each run, Pallas kernels for 7% -> 5%
where the time goes in v2:
time: 1610 us; the launch traced here: 1590 us
  waiting for transfers between devices  719 us (45%)
  matrix products  324 us (20%)
  starting transfers between devices  157 us (10%)
  other arithmetic  154 us (10%)
  Pallas kernels  114 us (7%)
  local copies, waits for them, and re-layouts  101 us (6%)
    all_gather x5, waiting for transfers between devices, gather(): return lax.all_gather(x, axis_name, axis=0, tiled=True)  195 us
    reduce_scatter x5, waiting for transfers between devices, scatter(): return lax.psum_scatter(x, axis_name, scatter_dimension=0, tiled=True)  130 us
    dot_general x5, matrix products, contract_last(): lax.dot_general(left, right, (((1,), (1,)), ((), ())), preferred_element_...  118 us
    ppermute x12, waiting for transfers between devices, fall(): lax.ppermute(send, 'sp', [(i, i - 1) for i in range(1, self.parts - step...  110 us
    dot_general x6, matrix products, contract_first(): lax.dot_general(left, right, (((0,), (0,)), ((), ())), preferred_element_...  108 us
    ppermute x18, waiting for transfers between devices, left(): lax.ppermute(x, axis_name, [(i, i - 1) for i in range(parts - count, part...  86.6 us
    ppermute x12, waiting for transfers between devices, right(): return lax.ppermute(x, axis_name, [(i, i + 1) for i in range(count)])  67 us
    pallas_call x2, Pallas kernels, attend_back(): pl.pallas_call(functools.partial(bwd_kernel, Z), grid_spec=pltpu.Prefetch...  55.2 us
  transfers between devices with their start and end apart: 70, of which 32 were waited for; matrix products, arithmetic and copies ran while one was open for 27% of the time, Pallas kernels for 5%

profile of v2, /device:TPU:0, one launch (start us, length us, event | category | flops | bytes accessed | tf_op | source)
XLA Modules:
  0.0 1585.1 jit_solution(9106908588004735630)
XLA Ops:
  64.0 22.3 %all-gather.6.cloned.1.call-done.w_ref = bf16[2560,1408]{1,0:T(8,128)(2,1)} async-done(((bf16[320,1408]{1,0:T(8,128)(2,1)}), bf16[2560,1408]{1,0:T(8,128)(2,1)}) %all-gather.6.cloned.1.call-update) | async-done | bytes 7208976 | tf_op jit(solution)/shard_map/all_gather | solution.py:259
  105.0 28.4 %collective-permute-done.refs_1_ = bf16[2,256,1280]{2,1,0:T(8,128)(2,1)S(1)} collective-permute-done((bf16[2,256,1280]{2,1,0:T(8,128)(2,1)S(1)}, bf16[2,256,1280]{2,1,0:T(8,128)(2,1)S(1)}, u32[]{:S(2)}, u32[]{:S(2)}) %collective-permute-start) | collective-permute-done | bytes 1310752 | tf_op jit(solution)/shard_map/ppermute | solution.py:414
  142.5 33.5 %all-gather.8.cloned.1.call-done.w_ref = bf16[2560,2560]{1,0:T(8,128)(2,1)} async-done(((bf16[320,2560]{1,0:T(8,128)(2,1)}), bf16[2560,2560]{1,0:T(8,128)(2,1)}) %all-gather.8.cloned.1.call-update) | async-done | bytes 13107216 | tf_op jit(solution)/shard_map/all_gather | solution.py:259
  206.3 35.3 %attend_fwd.1 = (bf16[2,256,2560]{2,1,0:T(8,128)(2,1)}, f32[2,32,256]{2,1,0:T(8,128)}) custom-call(s32[3]{0:T(128)} %pad_add_fusion.meta, bf16[2,256,2560]{2,1,0:T(8,128)(2,1)} %bitcast.258, bf16[2,256,1280]{2,1,0:T(8,128)(2,1)} %bitcast.257, bf16[2,256,1280]{2,1,0:T(8,128)(2,1)} %copy-done.33, bf16[2,256,1280]{2,1,0:T(8,128)(2,1)} %collective-permute-done.1.refs_2_, ...), custom_call_target="tpu_custom_call" | custom-call | tf_op jit(solution)/shard_map/attend_fwd/pallas_call | solution.py:98
  251.1 22.4 %all-gather.10.cloned.1.call-done = bf16[2560,2560]{1,0:T(8,128)(2,1)} async-done(((bf16[320,2560]{1,0:T(8,128)(2,1)}), bf16[2560,2560]{1,0:T(8,128)(2,1)}) %all-gather.10.cloned.1.call-update) | async-done | bytes 13107216 | tf_op jit(solution)/shard_map/all_gather | solution.py:259
  273.5 21.7 %multiply_reduce_fusion.3 = (f32[512]{0:T(512)S(1)}, f32[512,2560]{1,0:T(8,128)S(1)}) fusion(bf16[512,2560]{1,0:T(8,128)(2,1)} %bitcast.300, bf16[2560,2560]{1,0:T(8,128)(2,1)} %all-gather.10.cloned.1.call-done, bf16[2,256,2560]{2,1,0:T(8,128)(2,1)S(1)} %copy-done.20), kind=kOutput, calls=%fused_computation.38 | convolution fusion | flops 6716128768 | bytes 23595008 | tf_op jit(solution)/shard_map/dot_general | solution.py:428
  321.7 37.7 %collective-permute-done.6 = bf16[8,80,1792]{2,1,0:T(8,128)(2,1)} collective-permute-done((bf16[8,80,1792]{2,1,0:T(8,128)(2,1)}, bf16[8,80,1792]{2,1,0:T(8,128)(2,1)}, u32[]{:S(2)}, u32[]{:S(2)}) %collective-permute-start.6) | collective-permute-done | bytes 2293792 | tf_op jit(solution)/shard_map/ppermute | solution.py:326
  373.8 54.1 %all-gather.12.cloned.1.call-done = bf16[4096,2560]{1,0:T(8,128)(2,1)} async-done(((bf16[512,2560]{1,0:T(8,128)(2,1)}), bf16[4096,2560]{1,0:T(8,128)(2,1)}) %all-gather.12.cloned.1.call-update) | async-done | bytes 20971536 | tf_op jit(solution)/shard_map/all_gather | solution.py:259
  427.8 46.7 %fusion.67 = f32[4096,1792]{1,0:T(8,128)} fusion(bf16[4096,2560]{1,0:T(8,128)(2,1)} %all-gather.12.cloned.1.call-done, bf16[2560,1792]{1,0:T(8,128)(2,1)} %bitcast.24), kind=kOutput, calls=%fused_computation.185 | convolution fusion | flops 37580963840 | bytes 59506688 | tf_op jit(solution)/shard_map/dot_general | solution.py:437
  474.5 62.7 %all-gather.14.cloned.1.call-done = bf16[4096,2560]{1,0:T(8,128)(2,1)} async-done(((bf16[512,2560]{1,0:T(8,128)(2,1)}), bf16[4096,2560]{1,0:T(8,128)(2,1)}) %all-gather.14.cloned.1.call-update) | async-done | bytes 20971536 | tf_op jit(solution)/shard_map/all_gather | solution.py:259
  537.2 38.0 %multiply_convert_fusion = (bf16[4096,896]{1,0:T(8,128)(2,1)}, bf16[4096,896]{1,0:T(8,128)(2,1)}, bf16[4096,896]{1,0:T(8,128)(2,1)}) fusion(f32[4096,1792]{1,0:T(8,128)} %fusion.67, bf16[4096,2560]{1,0:T(8,128)(2,1)} %all-gather.14.cloned.1.call-done, f32[896,2560]{1,0:T(8,128)} %param.20), kind=kOutput, calls=%fused_computation.7 | convolution fusion | flops 18847825920 | bytes 81526784 | tf_op jit(solution)/shard_map/dot_general | solution.py:246
  575.2 24.5 %convolution_convert_fusion.7 = bf16[896,2560]{1,0:T(8,128)(2,1)S(1)} fusion(bf16[4096,896]{1,0:T(8,128)(2,1)} %get-tuple-element.80, bf16[4096,2560]{1,0:T(8,128)(2,1)} %all-gather.14.cloned.1.call-done), kind=kOutput, calls=%fused_computation.19 | convolution fusion | flops 18792775680 | bytes 32899072 | tf_op jit(solution)/shard_map/dot_general | solution.py:250
  607.1 46.6 %convolution_convert_fusion = bf16[4096,2560]{1,0:T(8,128)(2,1)} fusion(bf16[2560,1792]{1,0:T(8,128)(2,1)} %bitcast.24, bf16[4096,896]{1,0:T(8,128)(2,1)S(1)} %copy-done.68, bf16[4096,896]{1,0:T(8,128)(2,1)} %get-tuple-element.73), kind=kOutput, calls=%fused_computation | convolution fusion | flops 37620809728 | bytes 44826624 | tf_op jit(solution)/shard_map/dot_general | solution.py:246
  660.6 29.6 %convolution_convert_fusion.6 = bf16[2560,896]{1,0:T(8,128)(2,1)S(1)} fusion(bf16[4096,2560]{1,0:T(8,128)(2,1)} %all-gather.12.cloned.1.call-done, bf16[4096,896]{1,0:T(8,128)(2,1)} %get-tuple-element.73), kind=kOutput, calls=%fused_computation.18 | convolution fusion | flops 18792775680 | bytes 32899072 | tf_op jit(solution)/shard_map/dot_general | solution.py:250
  700.1 27.5 %convolution_convert_fusion.5 = bf16[2560,896]{1,0:T(8,128)(2,1)S(1)} fusion(bf16[4096,2560]{1,0:T(8,128)(2,1)} %all-gather.12.cloned.1.call-done, bf16[4096,896]{1,0:T(8,128)(2,1)} %get-tuple-element.76), kind=kOutput, calls=%fused_computation.17 | convolution fusion | flops 18792775680 | bytes 32899072 | tf_op jit(solution)/shard_map/dot_general | solution.py:250
  792.2 29.6 %convolution_convert_fusion.1 = bf16[4096,2560]{1,0:T(8,128)(2,1)} fusion(bf16[4096,896]{1,0:T(8,128)(2,1)} %get-tuple-element.80, f32[896,2560]{1,0:T(8,128)} %param.20), kind=kOutput, calls=%fused_computation.1 | convolution fusion | flops 18803261440 | bytes 37486592 | tf_op jit(solution)/shard_map/dot_general | solution.py:463
  898.8 21.0 %all-to-all-done.1 = bf16[8,2,80,896]{3,2,1,0:T(8,128)(2,1)S(1)} async-done(((bf16[8,2,80,896]{3,2,1,0:T(8,128)(2,1)}), bf16[8,2,80,896]{3,2,1,0:T(8,128)(2,1)S(1)}, u32[]{:S(2)}, u32[]{:S(2)}) %all-to-all-start.1) | async-done | bytes 2293792 | tf_op jit(solution)/shard_map/all_to_all | solution.py:476
  959.4 27.6 %attend_bwd.2 = (bf16[1,256,2560]{2,1,0:T(8,128)(2,1)}, bf16[1,256,1280]{2,1,0:T(8,128)(2,1)}, bf16[1,256,1280]{2,1,0:T(8,128)(2,1)}, bf16[1,256,1280]{2,1,0:T(8,128)(2,1)}, bf16[1,256,1280]{2,1,0:T(8,128)(2,1)}) custom-call(s32[2]{0:T(128)} %get-tuple-element.195.meta, bf16[1,256,2560]{2,1,0:T(8,128)(2,1)} %get-tuple-element.159.q_ref, ...), custom_call_target="tpu_custom_call" | custom-call | tf_op jit(solution)/shard_map/attend_bwd/pallas_call | solution.py:194
  988.1 27.7 %attend_bwd.3 = (bf16[1,256,2560]{2,1,0:T(8,128)(2,1)}, bf16[1,256,1280]{2,1,0:T(8,128)(2,1)}, bf16[1,256,1280]{2,1,0:T(8,128)(2,1)}, bf16[1,256,1280]{2,1,0:T(8,128)(2,1)}, bf16[1,256,1280]{2,1,0:T(8,128)(2,1)}) custom-call(s32[2]{0:T(128)} %get-tuple-element.196.meta, bf16[1,256,2560]{2,1,0:T(8,128)(2,1)} %get-tuple-element.160.q_ref, ...), custom_call_target="tpu_custom_call" | custom-call | tf_op jit(solution)/shard_map/attend_bwd/pallas_call | solution.py:194
  1031.0 27.6 %collective-permute-start.51 = (bf16[224,2560]{1,0:T(8,128)(2,1)}, bf16[224,2560]{1,0:T(8,128)(2,1)S(1)}, u32[]{:S(2)}, u32[]{:S(2)}) collective-permute-start(bf16[224,2560]{1,0:T(8,128)(2,1)} %get-tuple-element.122), channel_id=1, source_target_pairs={{0,1},{1,2},{2,3},{4,5},{5,6},{6,7},{8,9},{9,10},{10,11},{12,13},{... | collective-permute-start | bytes 3440648 | tf_op jit(solution)/shard_map/ppermute | solution.py:318
  1169.7 61.4 %collective-permute-done.31 = bf16[1,256,1280]{2,1,0:T(8,128)(2,1)S(1)} collective-permute-done((bf16[1,256,1280]{2,1,0:T(8,128)(2,1)S(1)}, bf16[1,256,1280]{2,1,0:T(8,128)(2,1)S(1)}, u32[]{:S(2)}, u32[]{:S(2)}) %collective-permute-start.31) | collective-permute-done | bytes 655392 | tf_op jit(solution)/shard_map/ppermute | solution.py:271
  1241.0 38.1 %reduce-scatter.10.cloned.1.call-done = bf16[320,2560]{1,0:T(8,128)(2,1)} async-done(((bf16[2560,2560]{1,0:T(8,128)(2,1)}), bf16[320,2560]{1,0:T(8,128)(2,1)}) %reduce-scatter.10.cloned.1.call-update) | async-done | bytes 1638416 | tf_op jit(solution)/shard_map/reduce_scatter | solution.py:263
  1326.9 91.8 %reduce-scatter.6.cloned.1.call-done = bf16[512,2560]{1,0:T(8,128)(2,1)} async-done(((bf16[4096,2560]{1,0:T(8,128)(2,1)}), bf16[512,2560]{1,0:T(8,128)(2,1)}) %reduce-scatter.6.cloned.1.call-update) | async-done | bytes 2621456 | tf_op jit(solution)/shard_map/reduce_scatter | solution.py:263
  1522.8 37.6 %all-reduce.5.cloned.1.call-done = bf16[320,1280]{1,0:T(8,128)(2,1)} async-done(((bf16[320,1280]{1,0:T(8,128)(2,1)}), bf16[320,1280]{1,0:T(8,128)(2,1)}) %all-reduce.5.cloned.1.call-update) | async-done | bytes 819216 | tf_op jit(solution)/shard_map/psum | solution.py:517
  (430 shorter events, 676.1 us)
Async XLA Ops:
  7.2 79.1 %all-gather.6.cloned.1.call-start = ((), (), s32[]{:S(2)}) async-start(), calls=%async_computation.7 | async-start | bytes 8110080 | tf_op jit(solution)/shard_map/all_gather | solution.py:259
  22.6 153.4 %all-gather.8.cloned.1.call-start = ((), (), s32[]{:S(2)}) async-start(), calls=%async_computation.8 | async-start | bytes 14745600 | tf_op jit(solution)/shard_map/all_gather | solution.py:259
  101.5 172.0 %all-gather.10.cloned.1.call-start = ((), (), s32[]{:S(2)}) async-start(), calls=%async_computation.9 | async-start | bytes 14745600 | tf_op jit(solution)/shard_map/all_gather | solution.py:259
  195.7 232.2 %all-gather.12.cloned.1.call-start = ((), (), s32[]{:S(2)}) async-start(), calls=%async_computation.10 | async-start | bytes 23592960 | tf_op jit(solution)/shard_map/all_gather | solution.py:259
  299.6 237.6 %all-gather.14.cloned.1.call-start = ((), (), s32[]{:S(2)}) async-start(), calls=%async_computation.11 | async-start | bytes 23592960 | tf_op jit(solution)/shard_map/all_gather | solution.py:259
  300.2 628.8 %reduce-scatter.8.cloned.1.call-start = ((), (), s32[]{:S(2)}) async-start(), calls=%async_computation.13 | async-start | bytes 23592960 | tf_op jit(solution)/shard_map/reduce_scatter | solution.py:263
  303.7 64.5 %collective-permute-start.8 = (bf16[8,80,1792]{2,1,0:T(8,128)(2,1)}, bf16[8,80,1792]{2,1,0:T(8,128)(2,1)}, u32[]{:S(2)}, u32[]{:S(2)}) collective-permute-start(bf16[8,80,1792]{2,1,0:T(8,128)(2,1)} %collective-permute-done.7), channel_id=1, source_target_pairs={{2,3},{6,7},{10,11},{14,15},{18,19},{22,23},{26,27},{30,31}} | collective-permute-start | bytes 6881288 | tf_op jit(solution)/shard_map/ppermute | solution.py:318
  752.5 69.4 %collective-permute-start.17 = (bf16[8,80,896]{2,1,0:T(8,128)(2,1)}, bf16[8,80,896]{2,1,0:T(8,128)(2,1)S(1)}, u32[]{:S(2)}, u32[]{:S(2)}) collective-permute-start(bf16[8,80,896]{2,1,0:T(8,128)(2,1)} %get-tuple-element.142), channel_id=1, source_target_pairs={{0,1},{1,2},{4,5},{5,6},{8,9},{9,10},{12,13},{13,14},{16,17},{17,1... | collective-permute-start | bytes 3440648 | tf_op jit(solution)/shard_map/ppermute | solution.py:267
  764.6 67.8 %collective-permute-start.23 = (bf16[8,80,896]{2,1,0:T(8,128)(2,1)}, bf16[8,80,896]{2,1,0:T(8,128)(2,1)}, u32[]{:S(2)}, u32[]{:S(2)}) collective-permute-start(bf16[8,80,896]{2,1,0:T(8,128)(2,1)} %get-tuple-element.138), channel_id=1, source_target_pairs={{0,1},{1,2},{4,5},{5,6},{8,9},{9,10},{12,13},{13,14},{16,17},{17,1... | collective-permute-start | bytes 3440648 | tf_op jit(solution)/shard_map/ppermute | solution.py:267
  891.2 349.8 %reduce-scatter.12.cloned.1.call-start = ((), (), s32[]{:S(2)}) async-start(), calls=%async_computation.15 | async-start | bytes 14745600 | tf_op jit(solution)/shard_map/reduce_scatter | solution.py:263
  922.0 65.0 %collective-permute-start.27 = (bf16[2,80,7168]{2,1,0:T(8,128)(2,1)}, bf16[2,80,7168]{2,1,0:T(8,128)(2,1)}, u32[]{:S(2)}, u32[]{:S(2)}) collective-permute-start(bf16[2,80,7168]{2,1,0:T(8,128)(2,1)} %bitcast.141), channel_id=1, source_target_pairs={{0,1},{1,2},{2,3},{4,5},{5,6},{6,7},{8,9},{9,10},{10,11},{12,13},{... | collective-permute-start | bytes 6881288 | tf_op jit(solution)/shard_map/ppermute | solution.py:318
  1029.4 249.6 %reduce-scatter.10.cloned.1.call-start = ((), (), s32[]{:S(2)}) async-start(), calls=%async_computation.14 | async-start | bytes 14745600 | tf_op jit(solution)/shard_map/reduce_scatter | solution.py:263
  1030.2 388.5 %reduce-scatter.6.cloned.1.call-start = ((), (), s32[]{:S(2)}) async-start(), calls=%async_computation.12 | async-start | bytes 23592960 | tf_op jit(solution)/shard_map/reduce_scatter | solution.py:263
  1030.9 476.8 %reduce-scatter.14.cloned.1.call-start = ((), (), s32[]{:S(2)}) async-start(), calls=%async_computation.16 | async-start | bytes 7372800 | tf_op jit(solution)/shard_map/reduce_scatter | solution.py:263
  1079.9 63.6 %collective-permute-start.55 = (bf16[224,2560]{1,0:T(8,128)(2,1)S(1)}, bf16[224,2560]{1,0:T(8,128)(2,1)S(1)}, u32[]{:S(2)}, u32[]{:S(2)}) collective-permute-start(bf16[224,2560]{1,0:T(8,128)(2,1)S(1)} %collective-permute-done.51), channel_id=1, source_target_pairs={{1,2},{2,3},{5,6},{6,7},{9,10},{10,11},{13,14},{14,15},{17,18},{18... | collective-permute-start | bytes 3440648 | tf_op jit(solution)/shard_map/ppermute | solution.py:318
  1107.3 216.2 %collective-permute-start.49 = (bf16[2,80,7168]{2,1,0:T(8,128)(2,1)}, bf16[2,80,7168]{2,1,0:T(8,128)(2,1)}, u32[]{:S(2)}, u32[]{:S(2)}) collective-permute-start(bf16[2,80,7168]{2,1,0:T(8,128)(2,1)} %collective-permute-done.27), channel_id=1, source_target_pairs={{1,2},{2,3},{5,6},{6,7},{9,10},{10,11},{13,14},{14,15},{17,18},{18... | collective-permute-start | bytes 6881288 | tf_op jit(solution)/shard_map/ppermute | solution.py:318
  1143.5 182.1 %collective-permute-start.47 = (bf16[2,80,7168]{2,1,0:T(8,128)(2,1)}, bf16[2,80,7168]{2,1,0:T(8,128)(2,1)}, u32[]{:S(2)}, u32[]{:S(2)}) collective-permute-start(bf16[2,80,7168]{2,1,0:T(8,128)(2,1)} %collective-permute-done.28), channel_id=1, source_target_pairs={{1,0},{2,1},{5,4},{6,5},{9,8},{10,9},{13,12},{14,13},{17,16},{18,1... | collective-permute-start | bytes 6881288 | tf_op jit(solution)/shard_map/ppermute | solution.py:326
  1165.0 66.0 %collective-permute-start.31 = (bf16[1,256,1280]{2,1,0:T(8,128)(2,1)S(1)}, bf16[1,256,1280]{2,1,0:T(8,128)(2,1)S(1)}, u32[]{:S(2)}, u32[]{:S(2)}) collective-permute-start(bf16[1,256,1280]{2,1,0:T(8,128)(2,1)S(1)} %add_convert_fusion.5), channel_id=1, source_target_pairs={{1,0},{2,1},{3,2},{5,4},{6,5},{7,6},{9,8},{10,9},{11,10},{13,12},{... | collective-permute-start | bytes 1966088 | tf_op jit(solution)/shard_map/ppermute | solution.py:271
  1166.5 73.4 %collective-permute-start.34 = (bf16[1,256,1280]{2,1,0:T(8,128)(2,1)S(1)}, bf16[1,256,1280]{2,1,0:T(8,128)(2,1)S(1)}, u32[]{:S(2)}, u32[]{:S(2)}) collective-permute-start(bf16[1,256,1280]{2,1,0:T(8,128)(2,1)S(1)} %add_convert_fusion.2), channel_id=1, source_target_pairs={{1,0},{2,1},{3,2},{5,4},{6,5},{7,6},{9,8},{10,9},{11,10},{13,12},{... | collective-permute-start | bytes 1966088 | tf_op jit(solution)/shard_map/ppermute | solution.py:271
  1294.2 266.3 %all-reduce.5.cloned.1.call-start = ((), (), s32[]{:S(2)}) async-start(), calls=%async_computation.17 | async-start | bytes 1638400 | tf_op jit(solution)/shard_map/psum | solution.py:517
  1294.2 129.1 %collective-permute-start.38 = (bf16[80,5120]{1,0:T(8,128)(2,1)}, bf16[80,5120]{1,0:T(8,128)(2,1)}, u32[]{:S(2)}, u32[]{:S(2)}) collective-permute-start(bf16[80,5120]{1,0:T(8,128)(2,1)} %get-tuple-element.156), channel_id=1, source_target_pairs={{3,2},{7,6},{11,10},{15,14},{19,18},{23,22},{27,26},{31,30}} | collective-permute-start | bytes 2457608 | tf_op jit(solution)/shard_map/ppermute | solution.py:271
  1306.2 117.1 %collective-permute-start.36 = (bf16[80,5120]{1,0:T(8,128)(2,1)}, bf16[80,5120]{1,0:T(8,128)(2,1)}, u32[]{:S(2)}, u32[]{:S(2)}) collective-permute-start(bf16[80,5120]{1,0:T(8,128)(2,1)} %fusion.41), channel_id=1, source_target_pairs={{0,1},{1,2},{4,5},{5,6},{8,9},{9,10},{12,13},{13,14},{16,17},{17,1... | collective-permute-start | bytes 2457608 | tf_op jit(solution)/shard_map/ppermute | solution.py:267
  1323.5 152.3 %collective-permute-start.50 = (bf16[2,80,7168]{2,1,0:T(8,128)(2,1)}, bf16[2,80,7168]{2,1,0:T(8,128)(2,1)}, u32[]{:S(2)}, u32[]{:S(2)}) collective-permute-start(bf16[2,80,7168]{2,1,0:T(8,128)(2,1)} %collective-permute-done.49), channel_id=1, source_target_pairs={{2,3},{6,7},{10,11},{14,15},{18,19},{22,23},{26,27},{30,31}} | collective-permute-start | bytes 6881288 | tf_op jit(solution)/shard_map/ppermute | solution.py:318
  1325.6 113.5 %collective-permute-start.48 = (bf16[2,80,7168]{2,1,0:T(8,128)(2,1)}, bf16[2,80,7168]{2,1,0:T(8,128)(2,1)}, u32[]{:S(2)}, u32[]{:S(2)}) collective-permute-start(bf16[2,80,7168]{2,1,0:T(8,128)(2,1)} %collective-permute-done.47), channel_id=1, source_target_pairs={{1,0},{5,4},{9,8},{13,12},{17,16},{21,20},{25,24},{29,28}} | collective-permute-start | bytes 6881288 | tf_op jit(solution)/shard_map/ppermute | solution.py:326
  (123 other events, 3135.3 us)
Sparse Core Ops, SparseCore 0:
  12.3 73.9 all-gather.5
  101.6 74.3 all-gather.7
  195.8 77.6 all-gather.9
  299.8 128.0 all-gather.11
  429.6 107.5 all-gather.13
  657.7 135.0 reduce-scatter.7
  1029.5 150.6 reduce-scatter.11
  1183.8 95.1 reduce-scatter.9
  1282.7 135.9 reduce-scatter.5
  1422.0 62.9 reduce-scatter.13
  1507.9 52.5 all-reduce.4
